TPU v7x, 512 devices: a whole 4x4x16 slice. The times are simulated.
512 devices in a mesh: dp: 8 (over z_hi, y), shard: 16 (over z_lo, core), seq: 4 (over x).
Axes of the slice: x: 4, y: 4, z: 16 (z_hi: 2, z_lo: 8; z = z_hi * 8 + z_lo), core: 2. Of those that a mesh axis runs over, the one named last changes fastest.
Arguments:
- qkv: bfloat16 [128, 196, 3, 2560], P(('dp', 'shard'), 'seq'), may hold values from -6 to 6
- hidden_in: bfloat16 [128, 196, 5120], P(('dp', 'shard'), 'seq'), may hold values from -6 to 6
- clips: bfloat16 [128, 4, 14, 14, 512], P(('dp', 'shard'), 'seq'), may hold values from -6 to 6
- reset: int32 [128], P(('dp', 'shard')), may hold values 0 or 1
- source_group: int32 [128], P(('dp', 'shard')), may hold values from 0 to 7
- step_index: int32 [128], P(('dp', 'shard')), may hold values from 0 to 34
- conv_weight: bfloat16 [2, 3, 3, 512, 16], replicated, may hold values from -0.0625 to 0.0625
- embed_weight: bfloat16 [64, 5120], replicated, may hold values from -0.75 to 0.75
- out_weight: bfloat16 [2560, 5120], P('seq', 'shard'), may hold values from -0.125 to 0.125
- gate_table: bfloat16 [35, 5120], replicated, may hold values from -8 to 8
Outputs:
- hidden_out: bfloat16 [128, 196, 5120], P(('dp', 'shard'), 'seq')
All inputs are finite; a program needn't handle non-finite values. No bound on the sum of `reset` on one device may be relied on, other than what follows from the above.
Results may differ from a plain program's by a relative error of at most 0.012.
Values may be sent and summed in bfloat16 or wider, within the bound.
A program may use at most 64 MiB of HBM per device.

v0:
```python
import math

import jax
import jax.numpy as jnp
from jax import lax
from jax.sharding import PartitionSpec as P

HD = 128


def passed_along(value, axis, steps):
    count = lax.axis_size(axis)
    first, last = (max(0, -steps), min(count, count - steps))
    return lax.ppermute(value, axis, [(source, source + steps) for source in range(first, last)])


def patch_tokens(latent):
    frames, grid_side, _, channels = latent.shape
    half_side = grid_side // 2
    grid_cells = latent.reshape(frames, half_side, 2, half_side, 2, channels)
    grid_cells = grid_cells.transpose(0, 1, 3, 2, 4, 5)
    return grid_cells.reshape(frames * half_side * half_side, 4 * channels)


def convolve(activated, previous, conv_weight):
    stacked = jnp.stack([previous, activated], axis=1)
    grid_side = activated.shape[1]
    padded = jnp.pad(stacked, ((0, 0), (0, 0), (1, 1), (1, 1), (0, 0)))
    tap_list = []
    for delta_t in range(2):
        for delta_y in range(3):
            for delta_x in range(3):
                tap_list.append(
                    padded[
                        :, delta_t, delta_y : delta_y + grid_side, delta_x : delta_x + grid_side, :
                    ]
                )
    columns = jnp.concatenate(tap_list, axis=-1)
    flat_columns = columns.reshape(-1, columns.shape[-1])
    weight_matrix = conv_weight.reshape(-1, conv_weight.shape[-1])
    latent = jnp.dot(flat_columns, weight_matrix, preferred_element_type=jnp.float32).astype(
        jnp.bfloat16
    )
    return latent.reshape(activated.shape[0], grid_side, grid_side, conv_weight.shape[-1])


def encode_frames(clip_block, conv_weight):
    activated = jax.nn.silu(clip_block.astype(jnp.float32)).astype(jnp.bfloat16)
    earlier = passed_along(activated, "seq", 1)
    previous = jnp.concatenate([earlier, activated[:-1]], axis=0)
    return convolve(activated, previous, conv_weight)


def attend_heads(qkv_block):
    item_count, seq_length, _, head_width = qkv_block.shape
    head_count = head_width // HD
    grouped = qkv_block.reshape(item_count, seq_length, 3, head_count, HD)
    scores = jnp.einsum(
        "nqhd,nkhd->nhqk", grouped[:, :, 0], grouped[:, :, 1], preferred_element_type=jnp.float32
    ) / math.sqrt(HD)
    highest = jnp.max(scores, axis=-1, keepdims=True)
    powers = jnp.exp(scores - highest)
    weights = (powers / jnp.sum(powers, axis=-1, keepdims=True)).astype(jnp.bfloat16)
    mixed = jnp.einsum(
        "nhqk,nkhd->nqhd", weights, grouped[:, :, 2], preferred_element_type=jnp.float32
    )
    return mixed.astype(jnp.bfloat16).reshape(item_count, seq_length, head_width)


def per_device(
    qkv,
    hidden_in,
    clips,
    reset,
    source_group,
    step_index,
    conv_weight,
    embed_weight,
    out_weight,
    gate_table,
):
    attended = attend_heads(lax.all_to_all(qkv, "seq", split_axis=3, concat_axis=1, tiled=True))
    head_rows = attended[0]
    terms = jnp.dot(
        head_rows,
        lax.all_gather(out_weight, "shard", axis=1, tiled=True),
        preferred_element_type=jnp.float32,
    )
    projected = lax.psum_scatter(
        terms.astype(jnp.bfloat16), "seq", scatter_dimension=0, tiled=True
    ).astype(jnp.float32)
    every_clip = lax.all_gather(clips, "dp", axis=0, tiled=True)
    chosen_clip = lax.dynamic_index_in_dim(every_clip, source_group[0], 0, keepdims=False)
    latent = encode_frames(chosen_clip, conv_weight)
    condition = jnp.dot(patch_tokens(latent), embed_weight, preferred_element_type=jnp.float32)
    gate_row = lax.dynamic_index_in_dim(gate_table, step_index[0], 0, keepdims=False).astype(
        jnp.float32
    )
    reset_flag = reset[0].astype(jnp.float32)
    residual = hidden_in[0].astype(jnp.float32)
    result = residual + reset_flag * condition + gate_row * projected
    return result.astype(jnp.bfloat16)[None]


def solution(mesh):
    placed = (
        P(("dp", "shard"), "seq", None, None),
        P(("dp", "shard"), "seq", None),
        P(("dp", "shard"), "seq", None, None, None),
        P(("dp", "shard")),
        P(("dp", "shard")),
        P(("dp", "shard")),
        P(),
        P(),
        P("seq", "shard"),
        P(),
    )
    return jax.shard_map(
        per_device,
        mesh=mesh,
        in_specs=placed,
        out_specs=P(("dp", "shard"), "seq", None),
        check_vma=False,
    )
```

profile of v0, /device:TPU:6, one launch (start us, length us, event | category | flops | bytes accessed | tf_op | source)
XLA Modules:
  0.0 282.9 jit_solution(17636946686232548468)
XLA Ops:
  6.5 0.7 all-gather.3.cloned.1.call-update
  7.3 0.7 all-gather.5.cloned.1.call-update
  8.0 3.1 %copy.24 = bf16[1,49,3,2560]{1,2,0,3:T(4,128)(2,1)S(1)} copy(bf16[1,49,3,2560]{3,1,2,0:T(8,128)(2,1)} %param.10) | data formatting | bytes 1505280 | tf_op args[0]
  11.1 4.2 %reshape.131 = bf16[4,2,47040]{2,1,0:T(2,128)(2,1)} reshape(bf16[2560,1,3,49]{3,2,1,0:T(4,128)(2,1)S(1)} %bitcast.81) | data formatting | bytes 1505280
  15.3 10.0 %all-to-all-start = ((bf16[4,2,47040]{2,1,0:T(2,128)(2,1)}), bf16[4,2,47040]{2,1,0:T(2,128)(2,1)}, u32[]{:S(2)}, u32[]{:S(2)}) async-start(bf16[4,2,47040]{2,1,0:T(2,128)(2,1)} %reshape.131), calls=%async_computation | async-start | bytes 1507328 | tf_op jit(solution)/shard_map/all_to_all | solution.py:82
  26.0 1.2 copy.21
  27.2 1.1 reshape.121
  29.6 1.3 dynamic-slice.4
  31.6 0.9 dynamic-slice_convert_fusion
  32.5 0.2 all-to-all-done
  32.7 4.4 %reshape.132 = bf16[2560,1,3,49]{3,2,1,0:T(4,128)(2,1)S(1)} reshape(bf16[4,2,47040]{2,1,0:T(2,128)(2,1)} %all-to-all-done) | data formatting | bytes 1505280
  37.1 2.5 copy.25
  39.6 1.9 reshape.123
  41.5 0.2 fusion.27
  41.7 1.5 fusion.29
  43.3 81.9 %all-gather.3.cloned.1.call-done = bf16[8,1,14,14,512]{4,3,2,1,0:T(8,128)(2,1)} async-done(((bf16[1,1,14,14,512]{4,3,2,1,0:T(8,128)(2,1)}), bf16[8,1,14,14,512]{4,3,2,1,0:T(8,128)(2,1)}) %all-gather.3.cloned.1.call-update) | async-done | bytes 1605648 | tf_op jit(solution)/shard_map/all_gather | solution.py:92
  125.2 1.1 fusion.20
  126.3 1.3 collective-permute-start
  127.6 1.6 fusion.5
  129.2 0.9 copy.30
  130.1 1.1 fusion.24
  131.2 0.8 concatenate.53
  131.9 2.3 collective-permute-done
  134.2 0.2 fusion.15
  134.4 1.5 fusion.28
  135.8 1.7 concatenate.40
  137.5 1.7 concatenate.41
  139.2 1.7 concatenate.42
  140.9 1.7 concatenate.43
  142.5 1.7 concatenate.45
  144.2 0.7 concatenate.46
  145.0 0.1 concatenate.48
  145.1 0.1 concatenate.49
  145.2 0.1 concatenate.50
  145.2 0.1 concatenate.51
  145.7 1.7 constant_dynamic-update-slice_fusion.17
  147.4 1.7 constant_dynamic-update-slice_fusion.16
  149.1 1.6 constant_dynamic-update-slice_fusion.15
  150.7 1.7 constant_dynamic-update-slice_fusion.14
  152.3 0.7 constant_dynamic-update-slice_fusion.13
  153.1 1.7 constant_dynamic-update-slice_fusion.12
  154.8 1.7 constant_dynamic-update-slice_fusion.11
  156.5 0.7 constant_dynamic-update-slice_fusion.10
  157.2 0.7 constant_dynamic-update-slice_fusion.9
  157.9 0.7 constant_dynamic-update-slice_fusion.8
  158.6 0.7 constant_dynamic-update-slice_fusion.7
  159.3 0.7 constant_dynamic-update-slice_fusion.6
  160.0 0.7 constant_dynamic-update-slice_fusion.5
  160.7 0.7 constant_dynamic-update-slice_fusion.4
  161.4 0.7 constant_dynamic-update-slice_fusion.3
  162.2 0.7 constant_dynamic-update-slice_fusion.2
  162.9 0.7 constant_dynamic-update-slice_fusion.1
  163.6 0.7 constant_dynamic-update-slice_fusion
  164.3 69.7 %all-gather.5.cloned.1.call-done = bf16[640,5120]{0,1:T(8,128)(2,1)} async-done(((bf16[640,320]{0,1:T(8,128)(2,1)}), bf16[640,5120]{0,1:T(8,128)(2,1)}) %all-gather.5.cloned.1.call-update) | async-done | bytes 6553616 | tf_op jit(solution)/shard_map/all_gather | solution.py:86
  234.0 5.5 %convolution_convert_fusion = bf16[196,5120]{1,0:T(8,128)(2,1)S(1)} fusion(bf16[196,640]{0,1:T(8,128)(2,1)S(1)} %bitcast.84, bf16[640,5120]{0,1:T(8,128)(2,1)} %all-gather.5.cloned.1.call-done), kind=kOutput, calls=%fused_computation.1 | convolution fusion | flops 1285509120 | bytes 8811520 | tf_op jit(solution)/shard_map/dot_general | solution.py:84
  239.5 26.0 %fusion = bf16[56,5120]{1,0:T(8,128)(2,1)S(1)} fusion(bf16[196,5120]{1,0:T(8,128)(2,1)S(1)} %convolution_convert_fusion), kind=kCustom, calls=%all-reduce-scatter | all-reduce-scatter fusion | flops 1146881 | bytes 2582528
  265.6 1.4 collective-permute-start.1
  267.0 3.1 %convolution_convert_fusion.2 = bf16[196,16]{0,1:T(8,128)(2,1)S(1)} fusion(bf16[196,9216]{1,0:T(8,128)(2,1)} %constant_dynamic-update-slice_fusion, bf16[9216,16]{0,1:T(8,128)(2,1)} %reshape.121), kind=kOutput, calls=%fused_computation.14 | convolution fusion | flops 57805888 | bytes 3913856 | tf_op jit(solution)/shard_map/dot_general | solution.py:41
  270.2 0.1 copy.22
  270.3 0.1 reshape_reshape.3
  270.4 0.1 reshape.122
  270.6 3.3 %collective-permute-done.1 = bf16[21,5120]{1,0:T(8,128)(2,1)S(1)} collective-permute-done((bf16[21,5120]{1,0:T(8,128)(2,1)S(1)}, bf16[21,5120]{1,0:T(8,128)(2,1)S(1)}, u32[]{:S(2)}, u32[]{:S(2)}) %collective-permute-start.1) | collective-permute-done | bytes 215072
  273.8 0.9 concatenate.59
  274.8 1.3 fusion.11
  (19 shorter events, 0.6 us)
Async XLA Ops:
  6.5 268.2 %copy-start = (bf16[64,5120]{1,0:T(8,128)(2,1)S(1)}, bf16[64,5120]{1,0:T(8,128)(2,1)}, u32[]{:S(2)}) copy-start(bf16[64,5120]{1,0:T(8,128)(2,1)} %param.17) | copy-start | bytes 1966084
  6.5 118.7 %all-gather.3.cloned.1.call-start = ((), (), s32[]{:S(2)}) async-start(), calls=%async_computation.1 | async-start | bytes 2064384 | tf_op jit(solution)/shard_map/all_gather | solution.py:92
  7.3 226.7 %all-gather.5.cloned.1.call-start = ((), (), s32[]{:S(2)}) async-start(), calls=%async_computation.2 | async-start | bytes 6963200 | tf_op jit(solution)/shard_map/all_gather | solution.py:86
  15.3 17.4 %all-to-all-start = ((bf16[4,2,47040]{2,1,0:T(2,128)(2,1)}), bf16[4,2,47040]{2,1,0:T(2,128)(2,1)}, u32[]{:S(2)}, u32[]{:S(2)}) async-start(bf16[4,2,47040]{2,1,0:T(2,128)(2,1)} %reshape.131), calls=%async_computation | async-start | bytes 1507328 | tf_op jit(solution)/shard_map/all_to_all | solution.py:82
  126.3 7.9 %collective-permute-start = (bf16[1,14,14,512]{3,2,1,0:T(8,128)(2,1)S(1)}, bf16[1,14,14,512]{3,2,1,0:T(8,128)(2,1)S(1)}, u32[]{:S(2)}, u32[]{:S(2)}) collective-permute-start(bf16[1,14,14,512]{3,2,1,0:T(8,128)(2,1)S(1)} %fusion.20), channel_id=1, source_target_pairs={{0,1},{1,2},{2,3},{4,5},{5,6},{6,7},{8,9},{9,10},{10,11},{12,13},{... | collective-permute-start | bytes 602120 | tf_op jit(solution)/shard_map/ppermute | solution.py:14
  145.4 15.4 %copy-start.1 = (bf16[196,512]{1,0:T(8,128)(2,1)S(1)}, bf16[196,512]{1,0:T(8,128)(2,1)}, u32[]{:S(2)}) copy-start(bf16[196,512]{1,0:T(8,128)(2,1)} %concatenate.53) | copy-start | bytes 602116
  153.1 80.9 %copy-start.3 = (bf16[1,196,5,128]{1,3,2,0:T(8,128)(2,1)S(1)}, bf16[1,196,5,128]{1,3,2,0:T(8,128)(2,1)}, u32[]{:S(2)}) copy-start(bf16[1,196,5,128]{1,3,2,0:T(8,128)(2,1)} %copy.30) | copy-start | bytes 752644
  265.5 9.2 %copy-start.2 = (bf16[1,49,5120]{2,1,0:T(8,128)(2,1)S(1)}, bf16[1,49,5120]{2,1,0:T(8,128)(2,1)}, u32[]{:S(2)}) copy-start(bf16[1,49,5120]{2,1,0:T(8,128)(2,1)} %param.11) | copy-start | bytes 1505284
  265.6 8.2 %collective-permute-start.1 = (bf16[21,5120]{1,0:T(8,128)(2,1)S(1)}, bf16[21,5120]{1,0:T(8,128)(2,1)S(1)}, u32[]{:S(2)}, u32[]{:S(2)}) collective-permute-start(bf16[21,5120]{1,0:T(8,128)(2,1)S(1)} %slice.99), channel_id=1, source_target_pairs={{0,1},{1,2},{2,3},{4,5},{5,6},{6,7},{8,9},{9,10},{10,11},{12,13},{... | collective-permute-start | bytes 645128
Sparse Core Ops, SparseCore 0:
  10.5 114.5 all-gather.2
  127.3 106.6 all-gather.4
where the time goes:
time: 285 us; the launch traced here: 283 us
  waiting for transfers between devices  159 us (56%)
  local copies, waits for them, and re-layouts  52.8 us (19%)
  blocking collectives  26 us (9%)
  between operations  16.3 us (6%)
  matrix products  13.1 us (5%)
  starting transfers between devices  12.8 us (4%)
  other arithmetic  3.26 us (1%)
    all_gather x1, waiting for transfers between devices, per_device(): every_clip = lax.all_gather(clips, 'dp', axis=0, tiled=True)  81.9 us
    all_gather x1, waiting for transfers between devices, per_device(): lax.all_gather(out_weight, 'shard', axis=1, tiled=True)  69.7 us
    unnamed x32, local copies, waits for them, and re-layouts  33 us
    unnamed x1, blocking collectives  26 us
    concatenate x19, local copies, waits for them, and re-layouts, convolve(): columns = jnp.concatenate(tap_list, axis=-1)  11.3 us
    all_to_all x1, starting transfers between devices, per_device(): lax.all_to_all(qkv, 'seq', split_axis=3, concat_axis=1, tiled=True)  10 us
  transfers between devices with their start and end apart: 5, of which 5 were waited for; matrix products, arithmetic and copies ran while one was open for 22% of the time, Pallas kernels for 0%

commit v1 on v0

v1 whole, which is shorter than its diff:
```python
import math

import jax
import jax.numpy as jnp
from jax import lax
from jax.experimental import pallas as pl
from jax.experimental.pallas import tpu as pltpu
from jax.sharding import PartitionSpec as P

MESH = pl.DeviceIdType.MESH
BF16, F32 = jnp.bfloat16, jnp.float32
HD = 128
HG = 5
GW = HG * HD
D = 5120
NB = 8
BW = D // NB
CW = BW // 2
ROWS = 48
MAIN = 4 * ROWS
ALL = MAIN + 16
ORDER = (0, 7, 1, 6, 2, 5, 3, 4)
NT = (((1,), (1,)), ((), ()))


def body(
    reset_ref, source_ref, step_ref, qkv_ref, hidden_ref, clip_ref, conv_ref, embed_ref, w_ref, gate_ref,
    out_ref,
    qkv_v, hidden_v, clip_v, conv_v, embed_v, gate_v, out_v,
    wg, heads, tail_out, tail_in, att, terms, recv, tsend, trecv, act, sh, bsend, brecv, packs, gate_row, patch,
    loc_sem, send_sem, head_sem, tail_sem, z_sem, y_sem, sib_sem, term_sem, tt_sem, b_sem, pz_sem, py_sem,
):
    g, s, x = lax.axis_index("dp"), lax.axis_index("shard"), lax.axis_index("seq")
    zh, y, zl, c = g // 4, g % 4, s // 2, s % 2
    z = zh * 8 + zl
    hy = y % 2

    def at_x(d):
        return {"seq": (x + d) % 4}

    def at_y(d):
        return {"dp": zh * 4 + (y + d) % 4}

    def at_z(d):
        zz = (z + d) % 16
        return {"dp": (zz // 8) * 4 + y, "shard": (zz % 8) * 2 + c}

    sibling = {"shard": zl * 2 + 1 - c}
    partner = {"dp": (g + 4) % 8}

    barrier = pltpu.get_barrier_semaphore()
    everyone = [at_x(1), at_x(2), at_x(3), at_z(1), at_z(15), at_y(1), at_y(2), at_y(3), sibling, partner]
    for dev in everyone:
        pl.semaphore_signal(barrier, inc=1, device_id=dev, device_id_type=MESH)

    locals_ = []

    def load(src, dst):
        copy = pltpu.make_async_copy(src, dst, loc_sem.at[len(locals_)])
        copy.start()
        locals_.append(copy)
        return copy

    sent = []

    def send(src, dst, sem, dev):
        copy = pltpu.make_async_remote_copy(
            src_ref=src, dst_ref=dst, send_sem=send_sem.at[len(sent)], recv_sem=sem, device_id=dev, device_id_type=MESH
        )
        copy.start()
        sent.append(copy)

    def arrived(dst, sem):
        pltpu.make_async_remote_copy(
            src_ref=dst, dst_ref=dst, send_sem=send_sem.at[0], recv_sem=sem, device_id=sibling, device_id_type=MESH
        ).wait_recv()

    def block_rows(rel, core):
        return pl.multiple_of(((zl + rel) % 8) * BW + core * CW, 16)

    def cols(rel):
        return pl.ds(pl.multiple_of(((zl + rel) % 8) * BW, 128), BW)

    def w_at(start, size):
        return wg.at[pl.ds(pl.multiple_of(start, 16), size), :]

    qkv_in = load(qkv_ref, qkv_v)
    own_heads = load(
        qkv_ref.at[:, pl.ds(0, ROWS), pl.ds(pl.multiple_of(x * GW, 128), GW)], heads.at[:, pl.ds(0, ROWS), :]
    )
    clip_in = load(clip_ref, clip_v)
    conv_in = load(conv_ref, conv_v)
    own_w = load(w_ref, w_at(block_rows(0, c), CW))
    embed_in = load(embed_ref, embed_v)
    gate_in = load(gate_ref, gate_v)
    hidden_in = load(hidden_ref, hidden_v)

    pl.semaphore_wait(barrier, len(everyone))

    for d in (1, 3, 2):
        send(
            qkv_ref.at[:, pl.ds(0, ROWS), pl.ds(pl.multiple_of(((x + d) % 4) * GW, 128), GW)],
            heads.at[:, pl.ds((4 - d) * ROWS, ROWS), :],
            head_sem.at[4 - d],
            at_x(d),
        )
    half = pl.ds(pl.multiple_of(hy * 160, 16), 160)
    for way, d in ((0, 1), (1, 15)):
        send(w_ref.at[half, :], w_at(block_rows(0, c) + hy * 160, 160), z_sem.at[way, 1], at_z(d))
    send(w_ref, w_at(block_rows(0, c), CW), sib_sem.at[0], sibling)

    qkv_in.wait()
    row16 = lax.broadcasted_iota(jnp.int32, (16, 4 * GW), 0)
    tails = [qkv_v[p, ROWS : ROWS + 1, :].astype(F32) for p in range(3)]
    tail_out[...] = jnp.where(
        row16 == 0, tails[0], jnp.where(row16 == 1, tails[1], jnp.where(row16 == 2, tails[2], 0.0))
    ).astype(BF16)
    for d in (1, 3, 2):
        send(
            tail_out.at[:, pl.ds(pl.multiple_of(((x + d) % 4) * GW, 128), GW)],
            tail_in.at[4 - d],
            tail_sem.at[4 - d],
            at_x(d),
        )

    def w_poll(k):
        for way, d in ((0, 1), (1, 15)):
            rel = (8 - k) if way == 0 else k
            first = block_rows(rel, c) + hy * 160
            if k < 4:
                arrived(w_at(first, 160), z_sem.at[way, k])
                if k < 3:
                    send(w_at(first, 160), w_at(first, 160), z_sem.at[way, k + 1], at_z(d))
                else:
                    q = first + 80 * way
                    send(w_at(q, 80), w_at(q, 80), z_sem.at[way, 4], at_z(d))
                send(w_at(first, 80), w_at(first, 80), y_sem.at[rel], at_y(1))
                send(w_at(first + 80, 80), w_at(first + 80, 80), y_sem.at[rel], at_y(3))
                send(w_at(first, 160), w_at(first, 160), sib_sem.at[rel], sibling)
            else:
                q = first + 80 * way
                arrived(w_at(q, 80), z_sem.at[way, 4])
                send(w_at(q, 80), w_at(q, 80), y_sem.at[4], at_y(1 if way == 0 else 3))
                send(w_at(q, 80), w_at(q, 80), sib_sem.at[4], sibling)

    def y_poll(rel):
        other = block_rows(rel, c) + (1 - hy) * 160
        arrived(w_at(other, 160), y_sem.at[rel])
        send(w_at(other, 160), w_at(other, 160), sib_sem.at[rel], sibling)

    clip_in.wait()
    conv_in.wait()
    raw = clip_v[...].astype(F32)
    act[:, 0:14, :] = raw / (1.0 + jnp.exp(-raw))
    act[:, 14:16, :] = jnp.zeros((14, 2, 512), F32)
    flat = act[...].reshape(224, 512)
    for k, value in enumerate((pltpu.roll(flat, 1, 0), flat, pltpu.roll(flat, 223, 0))):
        sh[k, 0:16, :] = jnp.zeros((16, 512), BF16)
        sh[k, 240:256, :] = jnp.zeros((16, 512), BF16)
        sh[k, 16:240, :] = value.astype(BF16)
    total = jnp.zeros((224, 128), F32)
    for dy in range(3):
        for dx in range(3):
            taps = jnp.concatenate([conv_v[1, dy, dx]] * 4 + [conv_v[0, dy, dx]] * 4, axis=0)
            total += lax.dot_general(sh[dx, dy * 16 : dy * 16 + 224, :], taps, NT, preferred_element_type=F32)
    cell = lax.broadcasted_iota(jnp.int32, (224, 128), 0)
    lane = lax.broadcasted_iota(jnp.int32, (224, 128), 1)
    parity = ((cell >> 4) & 1) * 2 + (cell & 1)
    spread = jnp.where(((lane >> 4) & 3) == parity, total, 0.0)
    token = lax.broadcasted_iota(jnp.int32, (64, 224), 0)
    cell = lax.broadcasted_iota(jnp.int32, (64, 224), 1)
    mine = (token == (cell >> 5) * 7 + ((cell & 15) >> 1)) & ((cell & 15) < 14)
    both = jnp.dot(
        mine.astype(F32), spread, precision=lax.Precision.HIGHEST, preferred_element_type=F32
    )
    low = lax.broadcasted_iota(jnp.int32, (32, 128), 1) < 64
    this_tap = jnp.where(low, both[0:32], pltpu.roll(both[32:64], 64, 1))
    bsend[...] = jnp.where(low, pltpu.roll(both[0:32], 64, 1), both[32:64])
    send(bsend, brecv, b_sem.at[0], at_x(1))

    w_poll(1)

    gate_in.wait()
    hot = lax.broadcasted_iota(jnp.int32, (16, 35), 1) == step_ref[0]
    gate_row[...] = jnp.dot(hot.astype(F32).astype(BF16), gate_v[...], preferred_element_type=F32)

    arrived(brecv, b_sem.at[0])
    packs[y, zh] = (this_tap + jnp.where(x > 0, brecv[...], 0.0)).astype(BF16)
    send(packs.at[y, zh], packs.at[y, zh], pz_sem.at[0], partner)

    w_poll(2)

    own_heads.wait()
    for d in (1, 2, 3):
        arrived(heads.at[:, pl.ds(d * ROWS, ROWS), :], head_sem.at[d])
        arrived(tail_in.at[d], tail_sem.at[d])
    tail_in[0] = tail_out[:, pl.ds(pl.multiple_of(x * GW, 128), GW)]
    row = lax.broadcasted_iota(jnp.int32, (16, GW), 0)
    ends = [tail_in[j].astype(F32) for j in range(4)]
    for p in range(3):
        value = jnp.zeros((16, GW), F32)
        for j in range(4):
            value = jnp.where(row == j, ends[j][p : p + 1, :], value)
        heads[p, MAIN:ALL, :] = value.astype(BF16)
    key_col = lax.broadcasted_iota(jnp.int32, (ALL, ALL), 1)
    for h in range(HG):
        at = slice(h * HD, (h + 1) * HD)
        scores = lax.dot_general(heads[0, :, at], heads[1, :, at], NT, preferred_element_type=F32)
        scores = jnp.where(key_col < 196, scores * (1.0 / math.sqrt(HD)), -1e30)
        powers = jnp.exp(scores - jnp.max(scores, axis=1, keepdims=True))
        weights = (powers / jnp.sum(powers, axis=1, keepdims=True)).astype(BF16)
        att[:, at] = jnp.dot(weights, heads[2, :, at], preferred_element_type=F32).astype(BF16)

    arrived(packs.at[y, 1 - zh], pz_sem.at[0])
    for d in (1, 3, 2):
        send(packs.at[y], packs.at[y], py_sem.at[4 - d], at_y(d))

    def project(i):
        rel = ORDER[i]
        arrived(w_at(block_rows(rel, 1 - c), CW), sib_sem.at[rel])
        rows = pl.ds(pl.multiple_of(((zl + rel) % 8) * BW, 16), BW)
        value = lax.dot_general(att[...], wg[rows, :], NT, preferred_element_type=F32)
        terms[i] = value[0:MAIN].astype(BF16)
        for j in range(4):
            for t in range(5):
                tsend[j, i * 5 + t : i * 5 + t + 1, :] = value[MAIN + j : MAIN + j + 1, t * 128 : (t + 1) * 128]
        for d in (1, 3, 2):
            send(terms.at[i, pl.ds(d * ROWS, ROWS), :], recv.at[4 - d, i], term_sem.at[4 - d, i], at_x(d))

    own_w.wait()
    w_poll(3)
    project(0)
    y_poll(7)
    y_poll(1)
    w_poll(4)
    project(1)
    y_poll(6)
    project(2)
    y_poll(2)
    project(3)
    y_poll(5)
    project(4)
    y_poll(3)
    project(5)
    y_poll(4)
    project(6)
    project(7)
    for d in (1, 3, 2):
        send(tsend.at[d], trecv.at[4 - d], tt_sem.at[4 - d], at_x(d))

    for d in (1, 2, 3):
        arrived(packs.at[(y + d) % 4], py_sem.at[d])
    chosen = jnp.zeros((32, 128), F32)
    for k in range(8):
        chosen = jnp.where(source_ref[0] == k, packs[k % 4, k // 4].astype(F32), chosen)
    patch[0:32, :] = chosen.astype(BF16)
    patch[32:64, :] = pltpu.roll(chosen, 64, 1).astype(BF16)
    embed_in.wait()
    hidden_in.wait()
    flag = reset_ref[0].astype(F32)
    patches = patch[:, 0:64]

    for i in range(NB):
        at = cols(ORDER[i])
        projected = terms[i, 0:ROWS, :].astype(F32)
        for d in (1, 3, 2):
            arrived(recv.at[d, i], term_sem.at[d, i])
            projected += recv[d, i].astype(F32)
        condition = jnp.dot(patches[0:ROWS], embed_v[:, at], preferred_element_type=F32)
        out_v[0:ROWS, at] = (
            hidden_v[0:ROWS, at].astype(F32) + flag * condition + gate_row[0:1, at] * projected
        ).astype(BF16)
    for d in (1, 2, 3):
        arrived(trecv.at[d], tt_sem.at[d])
    ends = tsend[0] + trecv[1] + trecv[2] + trecv[3]
    for i in range(NB):
        at = cols(ORDER[i])
        projected = jnp.concatenate([ends[i * 5 + t : i * 5 + t + 1, :] for t in range(5)], axis=1)
        condition = jnp.dot(patches[ROWS:64], embed_v[:, at], preferred_element_type=F32)[0:1]
        out_v[ROWS : ROWS + 1, at] = (
            hidden_v[ROWS : ROWS + 1, at].astype(F32) + flag * condition + gate_row[0:1, at] * projected
        ).astype(BF16)
    done = pltpu.make_async_copy(out_v, out_ref, loc_sem.at[len(locals_)])
    done.start()
    for copy in sent:
        copy.wait_send()
    done.wait()


def per_device(qkv, hidden_in, clips, reset, source_group, step_index, conv_weight, embed_weight, out_weight, gate_table):
    anywhere = pl.BlockSpec(memory_space=pl.ANY)
    scalar = pl.BlockSpec(memory_space=pltpu.SMEM)
    dma = pltpu.SemaphoreType.DMA
    result = pl.pallas_call(
        body,
        out_shape=jax.ShapeDtypeStruct((49, D), BF16),
        in_specs=[scalar] * 3 + [anywhere] * 7,
        out_specs=anywhere,
        scratch_shapes=[
            pltpu.VMEM((3, 49, 4 * GW), BF16),
            pltpu.VMEM((49, D), BF16),
            pltpu.VMEM((14, 14, 512), BF16),
            pltpu.VMEM((2, 3, 3, 16, 512), BF16),
            pltpu.VMEM((64, D), BF16),
            pltpu.VMEM((35, D), BF16),
            pltpu.VMEM((49, D), BF16),
            pltpu.VMEM((D, GW), BF16),
            pltpu.VMEM((3, ALL, GW), BF16),
            pltpu.VMEM((16, 4 * GW), BF16),
            pltpu.VMEM((4, 16, GW), BF16),
            pltpu.VMEM((ALL, GW), BF16),
            pltpu.VMEM((NB, MAIN, BW), BF16),
            pltpu.VMEM((4, NB, ROWS, BW), BF16),
            pltpu.VMEM((4, 40, 128), F32),
            pltpu.VMEM((4, 40, 128), F32),
            pltpu.VMEM((14, 16, 512), F32),
            pltpu.VMEM((3, 256, 512), BF16),
            pltpu.VMEM((32, 128), F32),
            pltpu.VMEM((32, 128), F32),
            pltpu.VMEM((4, 2, 32, 128), BF16),
            pltpu.VMEM((16, D), F32),
            pltpu.VMEM((64, 128), BF16),
            dma((9,)),
            dma((96,)),
            dma((4,)),
            dma((4,)),
            dma((2, 5)),
            dma((8,)),
            dma((8,)),
            dma((4, NB)),
            dma((4,)),
            dma((1,)),
            dma((1,)),
            dma((4,)),
        ],
        compiler_params=pltpu.CompilerParams(
            collective_id=0, has_side_effects=True, vmem_limit_bytes=48 * 1024 * 1024
        ),
        cost_estimate=pl.CostEstimate(flops=2_000_000_000, bytes_accessed=8_000_000, transcendentals=400_000),
    )(
        reset,
        source_group,
        step_index,
        qkv[0].transpose(1, 0, 2),
        hidden_in[0],
        clips[0, 0],
        conv_weight.transpose(0, 1, 2, 4, 3),
        embed_weight,
        out_weight.T,
        gate_table,
    )
    return result[None]


def solution(mesh):
    placed = (
        P(("dp", "shard"), "seq", None, None),
        P(("dp", "shard"), "seq", None),
        P(("dp", "shard"), "seq", None, None, None),
        P(("dp", "shard")),
        P(("dp", "shard")),
        P(("dp", "shard")),
        P(),
        P(),
        P("seq", "shard"),
        P(),
    )
    return jax.shard_map(
        per_device,
        mesh=mesh,
        in_specs=placed,
        out_specs=P(("dp", "shard"), "seq", None),
        check_vma=False,
    )
```

time: 285 us -> 70.4 us (0.25)
  the two profiles are of different devices: /device:TPU:6 before, /device:TPU:48 now
where the time goes in v1:
time: 70.4 us; the launch traced here: 70 us
  Pallas kernels  60 us (85%)
  local copies, waits for them, and re-layouts  8.01 us (11%)
  between operations  1.96 us (3%)
    pallas_call x1, Pallas kernels, per_device(): pl.pallas_call(body, out_shape=jax.ShapeDtypeStruct((49, D), BF16), in_sp...  60 us
    unnamed x15, local copies, waits for them, and re-layouts  8.01 us

profile of v1, /device:TPU:48, one launch (start us, length us, event | category | flops | bytes accessed | tf_op | source)
XLA Modules:
  0.0 70.0 jit_solution(13984444273473256739)
XLA Ops:
  1.9 0.0 copy-start
  2.0 1.1 %copy-done = bf16[1,49,3,2560]{3,1,2,0:T(8,128)(2,1)S(1)} copy-done((bf16[1,49,3,2560]{3,1,2,0:T(8,128)(2,1)S(1)}, bf16[1,49,3,2560]{3,1,2,0:T(8,128)(2,1)}, u32[]{:S(2)}) %copy-start) | copy-done | bytes 752664
  3.1 0.0 copy-start.1
  3.1 1.1 %copy-done.1 = bf16[64,5120]{1,0:T(8,128)(2,1)S(1)} copy-done((bf16[64,5120]{1,0:T(8,128)(2,1)S(1)}, bf16[64,5120]{1,0:T(8,128)(2,1)}, u32[]{:S(2)}) %copy-start.1) | copy-done | bytes 655384
  4.2 0.0 copy-start.2
  4.2 1.1 %copy-done.2 = bf16[1,49,5120]{2,1,0:T(8,128)(2,1)S(1)} copy-done((bf16[1,49,5120]{2,1,0:T(8,128)(2,1)S(1)}, bf16[1,49,5120]{2,1,0:T(8,128)(2,1)}, u32[]{:S(2)}) %copy-start.2) | copy-done | bytes 501784
  5.2 0.0 copy-start.3
  5.3 1.0 %copy-done.3 = bf16[640,320]{0,1:T(8,128)(2,1)S(1)} copy-done((bf16[640,320]{0,1:T(8,128)(2,1)S(1)}, bf16[640,320]{0,1:T(8,128)(2,1)}, u32[]{:S(2)}) %copy-start.3) | copy-done | bytes 409624
  6.3 0.0 copy-start.4
  6.3 1.0 %copy-done.4 = bf16[35,5120]{1,0:T(8,128)(2,1)S(1)} copy-done((bf16[35,5120]{1,0:T(8,128)(2,1)S(1)}, bf16[35,5120]{1,0:T(8,128)(2,1)}, u32[]{:S(2)}) %copy-start.4) | copy-done | bytes 358424
  7.3 0.0 copy-start.5
  7.3 1.0 %copy-done.5 = bf16[2,3,3,512,16]{3,4,2,1,0:T(8,128)(2,1)S(1)} copy-done((bf16[2,3,3,512,16]{3,4,2,1,0:T(8,128)(2,1)S(1)}, bf16[2,3,3,512,16]{3,4,2,1,0:T(8,128)(2,1)}, u32[]{:S(2)}) %copy-start.5) | copy-done | bytes 294936
  8.2 0.0 copy-start.6
  8.2 0.9 %copy-done.6 = bf16[1,1,14,14,512]{4,3,2,1,0:T(8,128)(2,1)S(1)} copy-done((bf16[1,1,14,14,512]{4,3,2,1,0:T(8,128)(2,1)S(1)}, bf16[1,1,14,14,512]{4,3,2,1,0:T(8,128)(2,1)}, u32[]{:S(2)}) %copy-start.6) | copy-done | bytes 200728
  9.2 60.0 %shard_map.100 = bf16[49,5120]{1,0:T(8,128)(2,1)S(1)} custom-call(s32[1]{0:T(128)S(6)} %copy.12.reset_ref, s32[1]{0:T(128)S(6)} %copy.13.source_ref, s32[1]{0:T(128)S(6)} %copy.14.step_ref, bf16[3,49,2560]{2,1,0:T(8,128)(2,1)S(1)} %bitcast.9, bf16[49,5120]{1,0:T(8,128)(2,1)S(1)} %bitcast.10, bf16[14,14,512]{2,1,0:T(8,128)(2,1)S(1)} %bitcast.13, ...), custom_call_target="tpu_custom_call" | custom-call | flops 2000000000 | bytes 8000000 | tf_op jit(solution)/shard_map/pallas_call | solution.py:294
  69.2 0.8 %copy.15 = bf16[1,49,5120]{2,1,0:T(8,128)(2,1)} copy(bf16[1,49,5120]{2,1,0:T(8,128)(2,1)S(1)} %bitcast.8) | data formatting | bytes 1003520
Async XLA Ops:
  1.9 1.2 %copy-start = (bf16[1,49,3,2560]{3,1,2,0:T(8,128)(2,1)S(1)}, bf16[1,49,3,2560]{3,1,2,0:T(8,128)(2,1)}, u32[]{:S(2)}) copy-start(bf16[1,49,3,2560]{3,1,2,0:T(8,128)(2,1)} %param.10) | copy-start | bytes 2257924
  3.1 1.1 %copy-start.1 = (bf16[64,5120]{1,0:T(8,128)(2,1)S(1)}, bf16[64,5120]{1,0:T(8,128)(2,1)}, u32[]{:S(2)}) copy-start(bf16[64,5120]{1,0:T(8,128)(2,1)} %embed_ref.1) | copy-start | bytes 1966084
  4.2 1.1 %copy-start.2 = (bf16[1,49,5120]{2,1,0:T(8,128)(2,1)S(1)}, bf16[1,49,5120]{2,1,0:T(8,128)(2,1)}, u32[]{:S(2)}) copy-start(bf16[1,49,5120]{2,1,0:T(8,128)(2,1)} %param.11) | copy-start | bytes 1505284
  5.2 1.0 %copy-start.3 = (bf16[640,320]{0,1:T(8,128)(2,1)S(1)}, bf16[640,320]{0,1:T(8,128)(2,1)}, u32[]{:S(2)}) copy-start(bf16[640,320]{0,1:T(8,128)(2,1)} %param.18) | copy-start | bytes 1228804
  6.3 1.0 %copy-start.4 = (bf16[35,5120]{1,0:T(8,128)(2,1)S(1)}, bf16[35,5120]{1,0:T(8,128)(2,1)}, u32[]{:S(2)}) copy-start(bf16[35,5120]{1,0:T(8,128)(2,1)} %gate_ref.1) | copy-start | bytes 1075204
  7.3 1.0 %copy-start.5 = (bf16[2,3,3,512,16]{3,4,2,1,0:T(8,128)(2,1)S(1)}, bf16[2,3,3,512,16]{3,4,2,1,0:T(8,128)(2,1)}, u32[]{:S(2)}) copy-start(bf16[2,3,3,512,16]{3,4,2,1,0:T(8,128)(2,1)} %param.16) | copy-start | bytes 884740
  8.2 0.9 %copy-start.6 = (bf16[1,1,14,14,512]{4,3,2,1,0:T(8,128)(2,1)S(1)}, bf16[1,1,14,14,512]{4,3,2,1,0:T(8,128)(2,1)}, u32[]{:S(2)}) copy-start(bf16[1,1,14,14,512]{4,3,2,1,0:T(8,128)(2,1)} %param.12) | copy-start | bytes 602116

commit v2 on v1

v2 whole, which is shorter than its diff:
```python
import math

import jax
import jax.numpy as jnp
from jax import lax
from jax.experimental import pallas as pl
from jax.experimental.pallas import tpu as pltpu
from jax.sharding import PartitionSpec as P

MESH = pl.DeviceIdType.MESH
BF16, F32 = jnp.bfloat16, jnp.float32
HD = 128
HG = 5
GW = HG * HD
D = 5120
NB = 8
BW = D // NB
CW = BW // 2
ROWS = 48
MAIN = 4 * ROWS
ALL = MAIN + 16
QR = CW // 4
QR0 = 48
CROSSING = 4
HALVES = ((0, 384), (384, 256))
NT = (((1,), (1,)), ((), ()))


def body(
    reset_ref, source_ref, step_ref, qkv_ref, hidden_ref, clip_ref, conv_ref, embed_ref, w_ref, gate_ref,
    out_ref,
    qkv_v, hidden_v, clip_v, conv_v, embed_v, gate_v, out_v,
    wg, heads, tail_out, tail_in, att, terms, cross, recv, tsend, trecv, act, sh, bsend, brecv, packs, midway, gate_row, patch,
    loc_sem, out_sem, w_out_sem, z_sem, y_sem, sib_sem, term_sem, cross_sem, in_sem,
):
    g, s, x = lax.axis_index("dp"), lax.axis_index("shard"), lax.axis_index("seq")
    zh, y, zl, c = g // 4, g % 4, s // 2, s % 2
    z = zh * 8 + zl

    def at_x(d):
        return {"seq": (x + d) % 4}

    def at_y(d):
        return {"dp": zh * 4 + (y + d) % 4}

    def at_z(d):
        zz = (z + d) % 16
        return {"dp": (zz // 8) * 4 + y, "shard": (zz % 8) * 2 + c}

    sibling = {"shard": zl * 2 + 1 - c}

    barrier = pltpu.get_barrier_semaphore()

    def greet(dev):
        pl.semaphore_signal(barrier, inc=1, device_id=dev, device_id_type=MESH)

    for dev in (at_x(1), at_x(2), at_x(3), at_y(1), at_y(2), at_y(3), sibling):
        greet(dev)
    pl.when(z < 15)(lambda: greet(at_z(1)))
    pl.when(z > 0)(lambda: greet(at_z(15)))

    locals_ = []

    def load(src, dst):
        copy = pltpu.make_async_copy(src, dst, loc_sem.at[len(locals_)])
        copy.start()
        locals_.append(copy)
        return copy

    def remote(src, dst, out, sem, dev):
        return pltpu.make_async_remote_copy(
            src_ref=src, dst_ref=dst, send_sem=out, recv_sem=sem, device_id=dev, device_id_type=MESH
        )

    def send(src, dst, out, sem, dev, when=None):
        if when is None:
            remote(src, dst, out, sem, dev).start()
        else:
            pl.when(when)(lambda: remote(src, dst, out, sem, dev).start())

    def arrived(dst, sem):
        remote(dst, dst, out_sem.at[0], sem, sibling).wait_recv()

    ends_of_w = []

    def left(src, out):
        remote(src, src, out, in_sem.at[0], sibling).wait_send()

    near = [-1, 1, -2, 2, -3, 3, 4]
    runs = {0: [1, 2, 3, 4, 5, 6, 7], 1: [-1, 1, 2, 3, 4, 5, 6], 2: [-1, 1, -2, 2, 3, 4, 5]}
    block = [zl]
    for i in range(7):
        off = jnp.int32(near[i])
        for at, run in runs.items():
            off = jnp.where(z == at, run[i], jnp.where(z == 15 - at, -run[i], off))
        block.append((zl + off + 8) % 8)

    def block_rows(b, core):
        return pl.multiple_of(b * BW + core * CW, 16)

    def cols(i):
        return pl.ds(pl.multiple_of(block[i] * BW, 128), BW)

    def w_at(start, size):
        return wg.at[pl.ds(pl.multiple_of(start, 16), size), :]

    qkv_in = load(qkv_ref, qkv_v)
    own_heads = load(
        qkv_ref.at[:, pl.ds(0, ROWS), pl.ds(pl.multiple_of(x * GW, 128), GW)], heads.at[:, pl.ds(0, ROWS), :]
    )
    clip_in = load(clip_ref, clip_v)
    conv_in = load(conv_ref, conv_v)
    own_w = load(w_ref, w_at(block_rows(zl, c), CW))
    embed_in = load(embed_ref, embed_v)
    gate_in = load(gate_ref, gate_v)
    hidden_in = load(hidden_ref, hidden_v)

    pl.semaphore_wait(barrier, 7 + jnp.where(z < 15, 1, 0) + jnp.where(z > 0, 1, 0))

    for d in (1, 3, 2):
        send(
            qkv_ref.at[:, pl.ds(0, ROWS), pl.ds(pl.multiple_of(((x + d) % 4) * GW, 128), GW)],
            heads.at[:, pl.ds((4 - d) * ROWS, ROWS), :],
            out_sem.at[0],
            in_sem.at[0],
            at_x(d),
        )
    quarter = pl.ds(pl.multiple_of(y * QR, 16), QR)
    for way in (0, 1):
        here = (z < 15) if way == 0 else (z > 0)
        send(
            w_ref.at[quarter, :],
            w_at(block_rows(zl, c) + y * QR, QR),
            w_out_sem.at[way],
            z_sem.at[way, 1],
            at_z(1 if way == 0 else 15),
            here,
        )
        ends_of_w.append((QR, w_out_sem.at[way], here))
    send(w_ref, w_at(block_rows(zl, c), CW), out_sem.at[1], sib_sem.at[zl], sibling)

    qkv_in.wait()
    row16 = lax.broadcasted_iota(jnp.int32, (16, 4 * GW), 0)
    tails = [qkv_v[p, ROWS : ROWS + 1, :].astype(F32) for p in range(3)]
    tail_out[...] = jnp.where(
        row16 == 0, tails[0], jnp.where(row16 == 1, tails[1], jnp.where(row16 == 2, tails[2], 0.0))
    ).astype(BF16)
    for d in (1, 3, 2):
        send(
            tail_out.at[:, pl.ds(pl.multiple_of(((x + d) % 4) * GW, 128), GW)],
            tail_in.at[pl.ds((4 - d) * 16, 16), :],
            out_sem.at[0],
            in_sem.at[1],
            at_x(d),
        )

    def comes(u, k):
        if k <= 3:
            return u >= k, None
        if k == 4:
            return u >= 12, (u >= 4) & (u < 12)
        return u >= 8 + k, None

    def w_step(k):
        todo = []
        for way in (0, 1):
            u = z if way == 0 else 15 - z
            b = (z + (8 - k if way == 0 else k)) % 8
            first = block_rows(b, c) + y * QR
            narrow = (0, QR0) if way == 0 else (QR0, QR - QR0)
            out = 2 * k + way if k <= 4 else 5 + k
            on = 13 + 2 * (k - 1) + way if k < 4 else 15 + k
            for full, here in zip((True, False), comes(u, k)):
                if here is None:
                    continue
                lo, size = (0, QR) if full else narrow
                piece = w_at(first + lo, size)
                pl.when(here)(lambda: arrived(piece, z_sem.at[way, k]))
                if full and k < 7:
                    for wide, then in zip((True, False), comes(u + 1, k + 1)):
                        if then is None:
                            continue
                        lo2, size2 = (0, QR) if wide else narrow
                        part = w_at(first + lo2, size2)
                        also = here & then & (u < 15)
                        send(part, part, w_out_sem.at[on], z_sem.at[way, k + 1], at_z(1 if way == 0 else 15), also)
                        ends_of_w.append((size2, w_out_sem.at[on], also))
                todo.append((piece, w_out_sem.at[out], b, here))
                ends_of_w.append((3 * size, w_out_sem.at[out], here))
        for piece, out, b, here in todo:
            for d in (1, 3, 2):
                send(piece, piece, out, y_sem.at[b], at_y(d), here)

    def y_all(i):
        b = block[i]
        arrived(w_at(0, 3 * QR), y_sem.at[b])
        piece = w_at(block_rows(b, c), CW)
        send(piece, piece, out_sem.at[1], sib_sem.at[b], sibling)

    clip_in.wait()
    conv_in.wait()
    raw = clip_v[...].astype(F32)
    act[:, 0:14, :] = raw / (1.0 + jnp.exp(-raw))
    act[:, 14:16, :] = jnp.zeros((14, 2, 512), F32)
    flat = act[...].reshape(224, 512)
    for k, value in enumerate((pltpu.roll(flat, 1, 0), flat, pltpu.roll(flat, 223, 0))):
        sh[k, 0:16, :] = jnp.zeros((16, 512), BF16)
        sh[k, 240:256, :] = jnp.zeros((16, 512), BF16)
        sh[k, 16:240, :] = value.astype(BF16)
    total = jnp.zeros((224, 128), F32)
    for dy in range(3):
        for dx in range(3):
            taps = jnp.concatenate([conv_v[1, dy, dx]] * 4 + [conv_v[0, dy, dx]] * 4, axis=0)
            total += lax.dot_general(sh[dx, dy * 16 : dy * 16 + 224, :], taps, NT, preferred_element_type=F32)
    cell = lax.broadcasted_iota(jnp.int32, (224, 128), 0)
    lane = lax.broadcasted_iota(jnp.int32, (224, 128), 1)
    parity = ((cell >> 4) & 1) * 2 + (cell & 1)
    spread = jnp.where(((lane >> 4) & 3) == parity, total, 0.0)
    token = lax.broadcasted_iota(jnp.int32, (64, 224), 0)
    cell = lax.broadcasted_iota(jnp.int32, (64, 224), 1)
    mine = (token == (cell >> 5) * 7 + ((cell & 15) >> 1)) & ((cell & 15) < 14)
    both = jnp.dot(
        mine.astype(F32), spread, precision=lax.Precision.HIGHEST, preferred_element_type=F32
    )
    low = lax.broadcasted_iota(jnp.int32, (32, 128), 1) < 64
    this_tap = jnp.where(low, both[0:32], pltpu.roll(both[32:64], 64, 1))
    bsend[...] = jnp.where(low, pltpu.roll(both[0:32], 64, 1), both[32:64])
    send(bsend, brecv, out_sem.at[2], in_sem.at[2], at_x(1))

    w_step(1)
    gate_in.wait()
    hot = lax.broadcasted_iota(jnp.int32, (16, 35), 1) == step_ref[0]
    gate_row[...] = jnp.dot(hot.astype(F32).astype(BF16), gate_v[...], preferred_element_type=F32)
    w_step(2)
    y_all(1)
    w_step(3)

    own_heads.wait()
    arrived(heads.at[:, pl.ds(ROWS, 3 * ROWS), :], in_sem.at[0])
    arrived(tail_in.at[pl.ds(16, 48), :], in_sem.at[1])
    tail_in[0:16, :] = tail_out[:, pl.ds(pl.multiple_of(x * GW, 128), GW)]
    row = lax.broadcasted_iota(jnp.int32, (16, GW), 0)
    ends = [tail_in[j * 16 : j * 16 + 16, :].astype(F32) for j in range(4)]
    for p in range(3):
        value = jnp.zeros((16, GW), F32)
        for j in range(4):
            value = jnp.where(row == j, ends[j][p : p + 1, :], value)
        heads[p, MAIN:ALL, :] = value.astype(BF16)
    key_col = lax.broadcasted_iota(jnp.int32, (ALL, ALL), 1)
    for h in range(HG):
        at = slice(h * HD, (h + 1) * HD)
        scores = lax.dot_general(heads[0, :, at], heads[1, :, at], NT, preferred_element_type=F32)
        scores = jnp.where(key_col < 196, scores * (1.0 / math.sqrt(HD)), -1e30)
        powers = jnp.exp(scores - jnp.max(scores, axis=1, keepdims=True))
        weights = (powers / jnp.sum(powers, axis=1, keepdims=True)).astype(BF16)
        att[:, at] = jnp.dot(weights, heads[2, :, at], preferred_element_type=F32).astype(BF16)

    def project(i):
        arrived(w_at(block_rows(block[i], 1 - c), CW), sib_sem.at[block[i]])
        rows = pl.ds(pl.multiple_of(block[i] * BW, 16), BW)
        value = lax.dot_general(att[...], wg[rows, :], NT, preferred_element_type=F32)
        terms[i] = value[0:MAIN].astype(BF16)
        for j in range(4):
            for t in range(5):
                tsend[j, i * 5 + t : i * 5 + t + 1, :] = value[MAIN + j : MAIN + j + 1, t * 128 : (t + 1) * 128]
        if i >= CROSSING:
            for d in (1, 3, 2):
                send(terms.at[i, pl.ds(d * ROWS, ROWS), :], recv.at[4 - d, i], out_sem.at[3], term_sem.at[i], at_x(d))
            return
        for way, (lo, size) in enumerate(HALVES):
            send(
                terms.at[i, pl.ds(2 * ROWS, ROWS), pl.ds(lo, size)],
                cross.at[i, :, pl.ds(lo, size)],
                out_sem.at[3],
                cross_sem.at[i],
                at_x(1 if way == 0 else 3),
            )

    def add_on(i):
        arrived(cross.at[i], cross_sem.at[i])
        for way, (lo, size) in enumerate(HALVES):
            d = 1 if way == 0 else 3
            mine = terms[i, d * ROWS : (d + 1) * ROWS, lo : lo + size].astype(F32)
            terms[i, d * ROWS : (d + 1) * ROWS, lo : lo + size] = (
                mine + cross[i, :, lo : lo + size].astype(F32)
            ).astype(BF16)
            send(terms.at[i, pl.ds(d * ROWS, ROWS), :], recv.at[4 - d, i], out_sem.at[3], term_sem.at[i], at_x(d))

    def pass_frame():
        arrived(brecv, in_sem.at[2])
        packs[y, zh] = (this_tap + jnp.where(x > 0, brecv[...], 0.0)).astype(BF16)
        for way, here in ((0, z < 8), (1, z >= 8)):
            send(packs.at[y, way], midway.at[way], out_sem.at[4], in_sem.at[3 + way], at_z(4 if way == 0 else 12), here)

    def pass_far():
        here = (z >= 4) & (z < 12)
        for way in (0, 1):
            pl.when(here)(lambda: arrived(midway.at[way], in_sem.at[3 + way]))
            send(midway.at[way], packs.at[y, way], out_sem.at[5], in_sem.at[5], at_z(4 if way == 0 else 12), here)

    def pass_patches():
        arrived(packs.at[y, 1 - zh], in_sem.at[5])
        for d in (1, 3, 2):
            send(packs.at[y], packs.at[y], out_sem.at[6], in_sem.at[6], at_y(d))

    def finish(i, patches, flag):
        at = cols(i)
        peers = (1, 3) if i < CROSSING else (1, 2, 3)
        arrived(recv.at[pl.ds(0, len(peers)), i], term_sem.at[i])
        projected = terms[i, 0:ROWS, :].astype(F32)
        for d in peers:
            projected += recv[d, i].astype(F32)
        condition = jnp.dot(patches[0:ROWS], embed_v[:, at], preferred_element_type=F32)
        out_v[0:ROWS, at] = (
            hidden_v[0:ROWS, at].astype(F32) + flag * condition + gate_row[0:1, at] * projected
        ).astype(BF16)

    own_w.wait()
    project(0)
    w_step(4)
    y_all(2)
    pass_frame()
    project(1)
    project(2)
    y_all(3)
    add_on(0)
    w_step(5)
    project(3)
    add_on(1)
    y_all(4)
    add_on(2)
    w_step(6)
    project(4)
    pass_far()
    add_on(3)
    y_all(5)
    w_step(7)
    project(5)
    y_all(6)
    project(6)
    pass_patches()
    y_all(7)
    project(7)
    for d in (1, 3, 2):
        send(tsend.at[d], trecv.at[4 - d], out_sem.at[7], in_sem.at[7], at_x(d))

    arrived(packs.at[pl.ds(0, 3)], in_sem.at[6])
    chosen = jnp.zeros((32, 128), F32)
    for k in range(8):
        chosen = jnp.where(source_ref[0] == k, packs[k % 4, k // 4].astype(F32), chosen)
    patch[0:32, :] = chosen.astype(BF16)
    patch[32:64, :] = pltpu.roll(chosen, 64, 1).astype(BF16)
    embed_in.wait()
    hidden_in.wait()
    flag = reset_ref[0].astype(F32)
    patches = patch[:, 0:64]

    for i in range(NB):
        finish(i, patches, flag)
    arrived(trecv.at[pl.ds(1, 3)], in_sem.at[7])
    ends = tsend[0] + trecv[1] + trecv[2] + trecv[3]
    for i in range(NB):
        at = cols(i)
        projected = jnp.concatenate([ends[i * 5 + t : i * 5 + t + 1, :] for t in range(5)], axis=1)
        condition = jnp.dot(patches[ROWS:64], embed_v[:, at], preferred_element_type=F32)[0:1]
        out_v[ROWS : ROWS + 1, at] = (
            hidden_v[ROWS : ROWS + 1, at].astype(F32) + flag * condition + gate_row[0:1, at] * projected
        ).astype(BF16)
    done = pltpu.make_async_copy(out_v, out_ref, loc_sem.at[len(locals_)])
    done.start()
    left(w_at(0, 9 * ROWS + 3 * 16), out_sem.at[0])
    left(w_at(0, 8 * CW), out_sem.at[1])
    left(bsend, out_sem.at[2])
    left(w_at(0, NB * 3 * ROWS), out_sem.at[3])
    left(packs.at[y, zh], out_sem.at[4])
    pl.when((z >= 4) & (z < 12))(lambda: left(midway, out_sem.at[5]))
    left(packs.at[pl.ds(0, 3)], out_sem.at[6])
    left(trecv.at[pl.ds(1, 3)], out_sem.at[7])
    for size, out, here in ends_of_w:
        pl.when(here)(lambda: left(w_at(0, size), out))
    done.wait()


def per_device(qkv, hidden_in, clips, reset, source_group, step_index, conv_weight, embed_weight, out_weight, gate_table):
    anywhere = pl.BlockSpec(memory_space=pl.ANY)
    scalar = pl.BlockSpec(memory_space=pltpu.SMEM)
    dma = pltpu.SemaphoreType.DMA
    result = pl.pallas_call(
        body,
        out_shape=jax.ShapeDtypeStruct((49, D), BF16),
        in_specs=[scalar] * 3 + [anywhere] * 7,
        out_specs=anywhere,
        scratch_shapes=[
            pltpu.VMEM((3, 49, 4 * GW), BF16),
            pltpu.VMEM((49, D), BF16),
            pltpu.VMEM((14, 14, 512), BF16),
            pltpu.VMEM((2, 3, 3, 16, 512), BF16),
            pltpu.VMEM((64, D), BF16),
            pltpu.VMEM((35, D), BF16),
            pltpu.VMEM((49, D), BF16),
            pltpu.VMEM((D, GW), BF16),
            pltpu.VMEM((3, ALL, GW), BF16),
            pltpu.VMEM((16, 4 * GW), BF16),
            pltpu.VMEM((64, GW), BF16),
            pltpu.VMEM((ALL, GW), BF16),
            pltpu.VMEM((NB, MAIN, BW), BF16),
            pltpu.VMEM((NB, ROWS, BW), BF16),
            pltpu.VMEM((4, NB, ROWS, BW), BF16),
            pltpu.VMEM((4, 40, 128), F32),
            pltpu.VMEM((4, 40, 128), F32),
            pltpu.VMEM((14, 16, 512), F32),
            pltpu.VMEM((3, 256, 512), BF16),
            pltpu.VMEM((32, 128), F32),
            pltpu.VMEM((32, 128), F32),
            pltpu.VMEM((4, 2, 32, 128), BF16),
            pltpu.VMEM((2, 32, 128), BF16),
            pltpu.VMEM((16, D), F32),
            pltpu.VMEM((64, 128), BF16),
            dma((9,)),
            dma((8,)),
            dma((22,)),
            dma((2, 8)),
            dma((8,)),
            dma((8,)),
            dma((NB,)),
            dma((CROSSING,)),
            dma((8,)),
        ],
        compiler_params=pltpu.CompilerParams(
            collective_id=0, has_side_effects=True, vmem_limit_bytes=63 * 1024 * 1024
        ),
        cost_estimate=pl.CostEstimate(flops=2_000_000_000, bytes_accessed=8_000_000, transcendentals=400_000),
    )(
        reset,
        source_group,
        step_index,
        qkv[0].transpose(1, 0, 2),
        hidden_in[0],
        clips[0, 0],
        conv_weight.transpose(0, 1, 2, 4, 3),
        embed_weight,
        out_weight.T,
        gate_table,
    )
    return result[None]


def solution(mesh):
    placed = (
        P(("dp", "shard"), "seq", None, None),
        P(("dp", "shard"), "seq", None),
        P(("dp", "shard"), "seq", None, None, None),
        P(("dp", "shard")),
        P(("dp", "shard")),
        P(("dp", "shard")),
        P(),
        P(),
        P("seq", "shard"),
        P(),
    )
    return jax.shard_map(
        per_device,
        mesh=mesh,
        in_specs=placed,
        out_specs=P(("dp", "shard"), "seq", None),
        check_vma=False,
    )
```

time: 70.4 us -> 60.1 us (0.85)
  the two profiles are of different devices: /device:TPU:48 before, /device:TPU:1 now
where the time goes in v2:
time: 60.1 us; the launch traced here: 59.9 us
  Pallas kernels  56 us (93%)
  between operations  1.95 us (3%)
  local copies, waits for them, and re-layouts  1.91 us (3%)
    pallas_call x1, Pallas kernels, per_device(): pl.pallas_call(body, out_shape=jax.ShapeDtypeStruct((49, D), BF16), in_sp...  56 us
    unnamed x1, local copies, waits for them, and re-layouts  1.91 us

profile of v2, /device:TPU:1, one launch (start us, length us, event | category | flops | bytes accessed | tf_op | source)
XLA Modules:
  0.0 59.9 jit_solution(7323945664536922921)
XLA Ops:
  1.9 56.0 %shard_map.100 = bf16[49,5120]{1,0:T(8,128)(2,1)} custom-call(s32[1]{0:T(128)S(6)} %copy.12.reset_ref, s32[1]{0:T(128)S(6)} %copy.13.source_ref, s32[1]{0:T(128)S(6)} %copy.14.step_ref, bf16[3,49,2560]{2,1,0:T(8,128)(2,1)} %bitcast.9, bf16[49,5120]{1,0:T(8,128)(2,1)} %bitcast.10, bf16[14,14,512]{2,1,0:T(8,128)(2,1)} %bitcast.13, ...), custom_call_target="tpu_custom_call" | custom-call | flops 2000000000 | bytes 8000000 | tf_op jit(solution)/shard_map/pallas_call | solution.py:388
  58.0 1.9 %copy.15 = bf16[1,49,5120]{2,1,0:T(8,128)(2,1)} copy(bf16[1,49,5120]{2,1,0:T(8,128)(2,1)} %bitcast.8) | data formatting | bytes 1003520

commit v3 on v2

v3 whole, which is shorter than its diff:
```python
import math

import jax
import jax.numpy as jnp
from jax import lax
from jax.experimental import pallas as pl
from jax.experimental.pallas import tpu as pltpu
from jax.sharding import PartitionSpec as P

MESH = pl.DeviceIdType.MESH
BF16, F32 = jnp.bfloat16, jnp.float32
HD = 128
HG = 5
GW = HG * HD
D = 5120
NB = 8
BW = D // NB
CW = BW // 2
ROWS = 48
MAIN = 4 * ROWS
ALL = MAIN + 16
QR = CW // 4
CROSSING = 7
HALVES = ((0, 384), (384, 256))
NT = (((1,), (1,)), ((), ()))


def body(
    reset_ref, source_ref, step_ref, qkv_ref, hidden_ref, clip_ref, conv_ref, embed_ref, w_ref, gate_ref,
    out_ref,
    qkv_v, hidden_v, clip_v, conv_v, embed_v, gate_v, out_v,
    wg, heads, tail_rows, tail_out, tail_in, att, terms, cross, recv, tsend, tail_terms, trecv, tail_sum, act, sh, bsend, brecv, packs, midway, gate_row, patch,
    loc_sem, out_sem, z_sem, y_sem, sib_sem, term_sem, cross_sem, in_sem,
):
    g, s, x = lax.axis_index("dp"), lax.axis_index("shard"), lax.axis_index("seq")
    zh, y, zl, c = g // 4, g % 4, s // 2, s % 2
    z = zh * 8 + zl

    def at_x(d):
        return {"seq": (x + d) % 4}

    def at_y(d):
        return {"dp": zh * 4 + (y + d) % 4}

    def at_z(d):
        zz = (z + d) % 16
        return {"dp": (zz // 8) * 4 + y, "shard": (zz % 8) * 2 + c}

    sibling = {"shard": zl * 2 + 1 - c}

    barrier = pltpu.get_barrier_semaphore()

    def greet(dev):
        pl.semaphore_signal(barrier, inc=1, device_id=dev, device_id_type=MESH)

    for dev in (at_x(1), at_x(2), at_x(3), at_y(1), at_y(2), at_y(3), sibling):
        greet(dev)
    greet(at_z(15))
    pl.when(z < 15)(lambda: greet(at_z(1)))

    locals_ = []

    def load(src, dst):
        copy = pltpu.make_async_copy(src, dst, loc_sem.at[len(locals_)])
        copy.start()
        locals_.append(copy)
        return copy

    def remote(src, dst, out, sem, dev):
        return pltpu.make_async_remote_copy(
            src_ref=src, dst_ref=dst, send_sem=out, recv_sem=sem, device_id=dev, device_id_type=MESH
        )

    def send(src, dst, out, sem, dev, when=None):
        if when is None:
            remote(src, dst, out, sem, dev).start()
        else:
            pl.when(when)(lambda: remote(src, dst, out, sem, dev).start())

    def arrived(dst, sem):
        remote(dst, dst, out_sem.at[0], sem, sibling).wait_recv()

    def left(src, out):
        remote(src, src, out, in_sem.at[0], sibling).wait_send()

    near = [-1, 1, -2, 2, -3, 3, 4]
    runs = {0: [1, 2, -1, 3, -2, -3, 4], 1: [-1, 1, 2, -2, 3, -3, 4], 2: [-1, 1, -2, 2, 3, -3, 4]}
    block = [zl]
    for i in range(7):
        off = jnp.int32(near[i])
        for at, run in runs.items():
            off = jnp.where(z == at, run[i], jnp.where(z == 15 - at, -run[i], off))
        block.append((zl + off + 8) % 8)

    def block_rows(b, core):
        return pl.multiple_of(b * BW + core * CW, 16)

    def cols(i):
        return pl.ds(pl.multiple_of(block[i] * BW, 128), BW)

    def w_at(start, size):
        return wg.at[pl.ds(pl.multiple_of(start, 16), size), :]

    qkv_in = load(qkv_ref, qkv_v)
    own_heads = load(
        qkv_ref.at[:, pl.ds(0, ROWS), pl.ds(pl.multiple_of(x * GW, 128), GW)], heads.at[:, pl.ds(0, ROWS), :]
    )
    clip_in = load(clip_ref, clip_v)
    conv_in = load(conv_ref, conv_v)
    own_w = load(w_ref, w_at(block_rows(zl, c), CW))
    embed_in = load(embed_ref, embed_v)
    gate_in = load(gate_ref, gate_v)
    hidden_in = load(hidden_ref, hidden_v)

    qkv_in.wait()
    tail_rows[...] = jnp.zeros_like(tail_rows)
    for p in range(3):
        last = qkv_v[p, ROWS : ROWS + 1, :].astype(F32)
        for t in range(4 * HG):
            at = (t // HG) * 16 + p * HG + t % HG
            tail_rows[at : at + 1, :] = last[:, t * HD : (t + 1) * HD]
    tail_out[...] = tail_rows[...].astype(BF16)
    pl.semaphore_wait(barrier, 8 + jnp.where(z > 0, 1, 0))

    for d in (1, 3, 2):
        send(
            tail_out.at[pl.ds(pl.multiple_of(((x + d) % 4) * 16, 16), 16), :],
            tail_in.at[pl.ds((4 - d) * 16, 16), :],
            out_sem.at[8],
            in_sem.at[1],
            at_x(d),
        )

    for part, (lo, size) in enumerate(HALVES):
        for d in (2, 1, 3):
            send(
                qkv_ref.at[:, pl.ds(0, ROWS), pl.ds(pl.multiple_of(((x + d) % 4) * GW + lo, 128), size)],
                heads.at[:, pl.ds((4 - d) * ROWS, ROWS), pl.ds(lo, size)],
                out_sem.at[0],
                in_sem.at[8 + part],
                at_x(d),
            )
    def own_piece(q, way, when):
        start = ((y + q) % 4) * QR
        send(
            w_ref.at[pl.ds(pl.multiple_of(start, 16), QR), :],
            w_at(block_rows(zl, c) + start, QR),
            out_sem.at[1],
            z_sem.at[way, 2 + q],
            at_z(1 if way == 0 else 15),
            when,
        )

    for q in (0, 1):
        own_piece(q, 0, None)
        own_piece(q, 1, z > 0)
    send(w_ref, w_at(block_rows(zl, c), CW), out_sem.at[1], sib_sem.at[zl], sibling)

    def w_piece(k, q, way):
        b = (z + (8 - k if way == 0 else k)) % 8
        return w_at(block_rows(b, c) + ((y + q) % 4) * QR, QR), b

    def pass_on(k, q, way, when):
        piece, _ = w_piece(k, q, way)
        send(piece, piece, out_sem.at[1], z_sem.at[way, 2 * k + 2 + q], at_z(1 if way == 0 else 15), when)

    def w_step(k, q, late):
        todo = []
        for way in (0, 1):
            if k == 4 and q != way:
                continue
            crosses = (z if way == 0 else 15 - z) < k
            here = crosses if late else jnp.logical_not(crosses)
            piece, b = w_piece(k, q, way)
            pl.when(here)(lambda: arrived(piece, z_sem.at[way, 2 * k + q]))
            if k < 3 or (k == 3 and q == way):
                pass_on(k, q, way, here & (z > 0) if way == 1 and k < 3 and not late else here)
            todo.append((piece, b, here))
        for piece, b, here in todo:
            send(piece, piece, out_sem.at[1], y_sem.at[q, b], at_y(1 if q == 0 else 3), here)
            send(piece, piece, out_sem.at[1], sib_sem.at[b], sibling, here)

    def w_back():
        for q in (0, 1):
            own_piece(q, 1, z == 0)
        for k in (1, 2):
            for q in (0, 1):
                pass_on(k, q, 1, z == 0)

    def y_near(i):
        for q, d in ((0, 3), (1, 2)):
            piece = w_at(block_rows(block[i], c) + ((y + d) % 4) * QR, QR)
            arrived(piece, y_sem.at[q, block[i]])
            send(piece, piece, out_sem.at[1], sib_sem.at[block[i]], sibling)

    clip_in.wait()
    conv_in.wait()
    raw = clip_v[...].astype(F32)
    act[:, 0:14, :] = raw / (1.0 + jnp.exp(-raw))
    act[:, 14:16, :] = jnp.zeros((14, 2, 512), F32)
    flat = act[...].reshape(224, 512)
    for k, value in enumerate((pltpu.roll(flat, 1, 0), flat, pltpu.roll(flat, 223, 0))):
        sh[k, 0:16, :] = jnp.zeros((16, 512), BF16)
        sh[k, 240:256, :] = jnp.zeros((16, 512), BF16)
        sh[k, 16:240, :] = value.astype(BF16)
    total = jnp.zeros((224, 128), F32)
    for dy in range(3):
        for dx in range(3):
            taps = jnp.concatenate([conv_v[1, dy, dx]] * 4 + [conv_v[0, dy, dx]] * 4, axis=0)
            total += lax.dot_general(sh[dx, dy * 16 : dy * 16 + 224, :], taps, NT, preferred_element_type=F32)
    cell = lax.broadcasted_iota(jnp.int32, (224, 128), 0)
    lane = lax.broadcasted_iota(jnp.int32, (224, 128), 1)
    parity = ((cell >> 4) & 1) * 2 + (cell & 1)
    spread = jnp.where(((lane >> 4) & 3) == parity, total, 0.0)
    token = lax.broadcasted_iota(jnp.int32, (64, 224), 0)
    cell = lax.broadcasted_iota(jnp.int32, (64, 224), 1)
    mine = (token == (cell >> 5) * 7 + ((cell & 15) >> 1)) & ((cell & 15) < 14)
    both = jnp.dot(
        mine.astype(F32), spread, precision=lax.Precision.HIGHEST, preferred_element_type=F32
    )
    low = lax.broadcasted_iota(jnp.int32, (32, 128), 1) < 64
    this_tap = jnp.where(low, both[0:32], pltpu.roll(both[32:64], 64, 1))
    bsend[...] = jnp.where(low, pltpu.roll(both[0:32], 64, 1), both[32:64])
    send(bsend, brecv, out_sem.at[2], in_sem.at[2], at_x(1))

    w_step(1, 0, False)
    gate_in.wait()
    hot = lax.broadcasted_iota(jnp.int32, (16, 35), 1) == step_ref[0]
    gate_row[...] = jnp.dot(hot.astype(F32).astype(BF16), gate_v[...], preferred_element_type=F32)

    own_heads.wait()
    arrived(tail_in.at[pl.ds(16, 48), :], in_sem.at[1])
    tail_in[0:16, :] = tail_out[pl.ds(pl.multiple_of(x * 16, 16), 16), :]
    tail_rows[...] = tail_in[...].astype(F32)
    row = lax.broadcasted_iota(jnp.int32, (16, HD), 0)
    for p in range(3):
        for t in range(HG):
            value = jnp.zeros((16, HD), F32)
            for j in range(4):
                at = j * 16 + p * HG + t
                value = jnp.where(row == j, tail_rows[at : at + 1, :], value)
            heads[p, MAIN:ALL, t * HD : (t + 1) * HD] = value.astype(BF16)
    key_col = lax.broadcasted_iota(jnp.int32, (ALL, ALL), 1)

    def attend(part):
        lo, size = HALVES[part]
        arrived(heads.at[:, pl.ds(ROWS, 3 * ROWS), pl.ds(lo, size)], in_sem.at[8 + part])
        for h in range(lo // HD, (lo + size) // HD):
            at = slice(h * HD, (h + 1) * HD)
            scores = lax.dot_general(heads[0, :, at], heads[1, :, at], NT, preferred_element_type=F32)
            scores = jnp.where(key_col < 196, scores * (1.0 / math.sqrt(HD)), -1e30)
            powers = jnp.exp(scores - jnp.max(scores, axis=1, keepdims=True))
            weights = (powers / jnp.sum(powers, axis=1, keepdims=True)).astype(BF16)
            att[:, at] = jnp.dot(weights, heads[2, :, at], preferred_element_type=F32).astype(BF16)

    tsend[:, 40:48, :] = jnp.zeros((4, 8, 128), F32)

    def halves(i):
        return HALVES if i % 2 == 0 else HALVES[::-1]

    def project(i):
        arrived(w_at(block_rows(block[i], 1 - c), CW), sib_sem.at[block[i]])
        rows = pl.ds(pl.multiple_of(block[i] * BW, 16), BW)
        value = lax.dot_general(att[...], wg[rows, :], NT, preferred_element_type=F32)
        terms[i] = value[0:MAIN].astype(BF16)
        for j in range(4):
            for t in range(5):
                tsend[j, i * 5 + t : i * 5 + t + 1, :] = value[MAIN + j : MAIN + j + 1, t * 128 : (t + 1) * 128]
        if i >= CROSSING:
            for d in (1, 3, 2):
                send(terms.at[i, pl.ds(d * ROWS, ROWS), :], recv.at[4 - d, i], out_sem.at[3], term_sem.at[i], at_x(d))
            return
        for way, (lo, size) in enumerate(halves(i)):
            send(
                terms.at[i, pl.ds(2 * ROWS, ROWS), pl.ds(lo, size)],
                cross.at[i, :, pl.ds(lo, size)],
                out_sem.at[3],
                cross_sem.at[i],
                at_x(1 if way == 0 else 3),
            )

    def add_on(i):
        arrived(cross.at[i], cross_sem.at[i])
        for way, (lo, size) in enumerate(halves(i)):
            d = 1 if way == 0 else 3
            mine = terms[i, d * ROWS : (d + 1) * ROWS, lo : lo + size].astype(F32)
            terms[i, d * ROWS : (d + 1) * ROWS, lo : lo + size] = (
                mine + cross[i, :, lo : lo + size].astype(F32)
            ).astype(BF16)
            send(terms.at[i, pl.ds(d * ROWS, ROWS), :], recv.at[4 - d, i], out_sem.at[3], term_sem.at[i], at_x(d))

    def pass_frame():
        arrived(brecv, in_sem.at[2])
        packs[y, zh] = (this_tap + jnp.where(x > 0, brecv[...], 0.0)).astype(BF16)
        for way, here in ((0, z < 8), (1, z >= 8)):
            send(packs.at[y, way], midway.at[way], out_sem.at[4], in_sem.at[3 + way], at_z(4 if way == 0 else 12), here)

    def pass_far():
        here = (z >= 4) & (z < 12)
        for way in (0, 1):
            pl.when(here)(lambda: arrived(midway.at[way], in_sem.at[3 + way]))
            send(midway.at[way], packs.at[y, way], out_sem.at[5], in_sem.at[5], at_z(4 if way == 0 else 12), here)

    def pass_patches():
        arrived(packs.at[y, 1 - zh], in_sem.at[5])
        for d in (1, 3, 2):
            send(packs.at[y], packs.at[y], out_sem.at[6], in_sem.at[6], at_y(d))

    def choose_patches():
        arrived(packs.at[pl.ds(0, 3)], in_sem.at[6])
        chosen = jnp.zeros((32, 128), F32)
        for k in range(8):
            chosen = jnp.where(source_ref[0] == k, packs[k % 4, k // 4].astype(F32), chosen)
        patch[0:32, :] = chosen.astype(BF16)
        patch[32:64, :] = pltpu.roll(chosen, 64, 1).astype(BF16)

    outs = []

    def finish(i):
        at = cols(i)
        peers = (1, 3) if i < CROSSING else (1, 2, 3)
        arrived(recv.at[pl.ds(0, len(peers)), i], term_sem.at[i])
        projected = terms[i, 0:ROWS, :].astype(F32)
        for d in peers:
            projected += recv[d, i].astype(F32)
        last = jnp.concatenate([tail_sum[i * 5 + t : i * 5 + t + 1, :] for t in range(5)], axis=1)
        projected = jnp.concatenate([projected, last], axis=0)
        condition = jnp.dot(patch[:, 0:64], embed_v[:, at], preferred_element_type=F32)[0 : ROWS + 1]
        out_v[i] = (
            hidden_v[:, at].astype(F32) + reset_ref[0].astype(F32) * condition + gate_row[0:1, at] * projected
        ).astype(BF16)
        copy = pltpu.make_async_copy(out_v.at[i], out_ref.at[:, at], loc_sem.at[len(locals_) + i])
        copy.start()
        outs.append(copy)

    def send_tails(lo, size, k):
        tail_terms[:, lo : lo + size, :] = tsend[:, lo : lo + size, :].astype(BF16)
        for d in (1, 3, 2):
            send(
                tail_terms.at[d, pl.ds(lo, size), :],
                trecv.at[4 - d, pl.ds(lo, size), :],
                out_sem.at[7],
                in_sem.at[k],
                at_x(d),
            )

    def sum_tails(lo, size, k):
        arrived(trecv.at[pl.ds(1, 3), pl.ds(lo, size), :], in_sem.at[k])
        value = tsend[0, lo : lo + size, :]
        for d in (1, 2, 3):
            value += trecv[d, lo : lo + size, :].astype(F32)
        tail_sum[lo : lo + size, :] = value

    w_step(1, 1, False)
    attend(0)
    w_step(2, 0, False)
    y_near(1)
    w_step(2, 1, False)
    w_step(1, 0, True)
    w_back()
    attend(1)
    own_w.wait()
    project(0)
    w_step(3, 0, False)
    pass_frame()
    w_step(1, 1, True)
    y_near(2)
    project(1)
    w_step(3, 1, False)
    w_step(2, 0, True)
    y_near(3)
    w_step(2, 1, True)
    project(2)
    add_on(0)
    y_near(4)
    w_step(3, 0, True)
    project(3)
    add_on(1)
    w_step(4, 0, False)
    w_step(4, 1, False)
    w_step(3, 1, True)
    y_near(5)
    project(4)
    add_on(2)
    pass_far()
    w_step(4, 0, True)
    w_step(4, 1, True)
    y_near(6)
    project(5)
    add_on(3)
    y_near(7)
    project(6)
    send_tails(0, 32, 7)
    add_on(4)
    pass_patches()
    project(7)
    add_on(5)
    send_tails(32, 16, 10)
    add_on(6)
    choose_patches()
    embed_in.wait()
    hidden_in.wait()
    sum_tails(0, 32, 7)
    finish(0)
    finish(1)
    finish(2)
    finish(3)
    finish(4)
    finish(5)
    sum_tails(32, 16, 10)
    finish(6)
    finish(7)
    left(w_at(0, 9 * ROWS), out_sem.at[0])
    left(w_at(0, CW + 56 * QR), out_sem.at[1])
    left(bsend, out_sem.at[2])
    left(w_at(0, NB * 3 * ROWS), out_sem.at[3])
    left(packs.at[y, zh], out_sem.at[4])
    pl.when((z >= 4) & (z < 12))(lambda: left(midway, out_sem.at[5]))
    left(packs.at[pl.ds(0, 3)], out_sem.at[6])
    left(trecv.at[pl.ds(1, 3)], out_sem.at[7])
    left(tail_in.at[pl.ds(16, 48), :], out_sem.at[8])
    for copy in outs:
        copy.wait()


def per_device(qkv, hidden_in, clips, reset, source_group, step_index, conv_weight, embed_weight, out_weight, gate_table):
    anywhere = pl.BlockSpec(memory_space=pl.ANY)
    scalar = pl.BlockSpec(memory_space=pltpu.SMEM)
    dma = pltpu.SemaphoreType.DMA
    result = pl.pallas_call(
        body,
        out_shape=jax.ShapeDtypeStruct((49, D), BF16),
        in_specs=[scalar] * 3 + [anywhere] * 7,
        out_specs=anywhere,
        scratch_shapes=[
            pltpu.VMEM((3, 49, 4 * GW), BF16),
            pltpu.VMEM((49, D), BF16),
            pltpu.VMEM((14, 14, 512), BF16),
            pltpu.VMEM((2, 3, 3, 16, 512), BF16),
            pltpu.VMEM((64, D), BF16),
            pltpu.VMEM((35, D), BF16),
            pltpu.VMEM((NB, 49, BW), BF16),
            pltpu.VMEM((D, GW), BF16),
            pltpu.VMEM((3, ALL, GW), BF16),
            pltpu.VMEM((64, HD), F32),
            pltpu.VMEM((64, HD), BF16),
            pltpu.VMEM((64, HD), BF16),
            pltpu.VMEM((ALL, GW), BF16),
            pltpu.VMEM((NB, MAIN, BW), BF16),
            pltpu.VMEM((NB, ROWS, BW), BF16),
            pltpu.VMEM((4, NB, ROWS, BW), BF16),
            pltpu.VMEM((4, 48, 128), F32),
            pltpu.VMEM((4, 48, 128), BF16),
            pltpu.VMEM((4, 48, 128), BF16),
            pltpu.VMEM((48, 128), F32),
            pltpu.VMEM((14, 16, 512), F32),
            pltpu.VMEM((3, 256, 512), BF16),
            pltpu.VMEM((32, 128), F32),
            pltpu.VMEM((32, 128), F32),
            pltpu.VMEM((4, 2, 32, 128), BF16),
            pltpu.VMEM((2, 32, 128), BF16),
            pltpu.VMEM((16, D), F32),
            pltpu.VMEM((64, 128), BF16),
            dma((16,)),
            dma((9,)),
            dma((2, 10)),
            dma((2, 8)),
            dma((8,)),
            dma((NB,)),
            dma((CROSSING,)),
            dma((11,)),
        ],
        compiler_params=pltpu.CompilerParams(
            collective_id=0, has_side_effects=True, vmem_limit_bytes=63 * 1024 * 1024
        ),
        cost_estimate=pl.CostEstimate(flops=2_000_000_000, bytes_accessed=8_000_000, transcendentals=400_000),
    )(
        reset,
        source_group,
        step_index,
        qkv[0].transpose(1, 0, 2),
        hidden_in[0],
        clips[0, 0],
        conv_weight.transpose(0, 1, 2, 4, 3),
        embed_weight,
        out_weight.T,
        gate_table,
    )
    return result[None]


def solution(mesh):
    placed = (
        P(("dp", "shard"), "seq", None, None),
        P(("dp", "shard"), "seq", None),
        P(("dp", "shard"), "seq", None, None, None),
        P(("dp", "shard")),
        P(("dp", "shard")),
        P(("dp", "shard")),
        P(),
        P(),
        P("seq", "shard"),
        P(),
    )
    return jax.shard_map(
        per_device,
        mesh=mesh,
        in_specs=placed,
        out_specs=P(("dp", "shard"), "seq", None),
        check_vma=False,
    )
```

time: 60.1 us -> 53.6 us (0.89)
  the two profiles are of different devices: /device:TPU:1 before, /device:TPU:32 now
where the time goes in v3:
time: 53.6 us; the launch traced here: 53.5 us
  Pallas kernels  49.6 us (93%)
  between operations  1.95 us (4%)
  local copies, waits for them, and re-layouts  1.91 us (4%)
    pallas_call x1, Pallas kernels, per_device(): pl.pallas_call(body, out_shape=jax.ShapeDtypeStruct((49, D), BF16), in_sp...  49.6 us
    unnamed x1, local copies, waits for them, and re-layouts  1.91 us

profile of v3, /device:TPU:32, one launch (start us, length us, event | category | flops | bytes accessed | tf_op | source)
XLA Modules:
  0.0 53.5 jit_solution(3731395534554827060)
XLA Ops:
  1.9 49.6 %shard_map.100 = bf16[49,5120]{1,0:T(8,128)(2,1)} custom-call(s32[1]{0:T(128)S(6)} %copy.12.reset_ref, s32[1]{0:T(128)S(6)} %copy.13.source_ref, s32[1]{0:T(128)S(6)} %copy.14.step_ref, bf16[3,49,2560]{2,1,0:T(8,128)(2,1)} %bitcast.9, bf16[49,5120]{1,0:T(8,128)(2,1)} %bitcast.10, bf16[14,14,512]{2,1,0:T(8,128)(2,1)} %bitcast.13, ...), custom_call_target="tpu_custom_call" | custom-call | flops 2000000000 | bytes 8000000 | tf_op jit(solution)/shard_map/pallas_call | solution.py:430
  51.5 1.9 %copy.15 = bf16[1,49,5120]{2,1,0:T(8,128)(2,1)} copy(bf16[1,49,5120]{2,1,0:T(8,128)(2,1)} %bitcast.8) | data formatting | bytes 1003520

commit v4 on v3

--- a/solution.py
+++ b/solution.py
@@ -20,13 +20,13 @@
 MAIN = 4 * ROWS
 ALL = MAIN + 16
 QR = CW // 4
-CROSSING = 7
+CROSSING = (3, 4, 5, 6)
 HALVES = ((0, 384), (384, 256))
 NT = (((1,), (1,)), ((), ()))
 
 
 def body(
-    reset_ref, source_ref, step_ref, qkv_ref, hidden_ref, clip_ref, conv_ref, embed_ref, w_ref, gate_ref,
+    scalars, qkv_ref, hidden_ref, clip_ref, conv_ref, embed_ref, w_ref, gate_ref,
     out_ref,
     qkv_v, hidden_v, clip_v, conv_v, embed_v, gate_v, out_v,
     wg, heads, tail_rows, tail_out, tail_in, att, terms, cross, recv, tsend, tail_terms, trecv, tail_sum, act, sh, bsend, brecv, packs, midway, gate_row, patch,
@@ -112,26 +112,10 @@
     gate_in = load(gate_ref, gate_v)
     hidden_in = load(hidden_ref, hidden_v)
 
-    qkv_in.wait()
-    tail_rows[...] = jnp.zeros_like(tail_rows)
-    for p in range(3):
-        last = qkv_v[p, ROWS : ROWS + 1, :].astype(F32)
-        for t in range(4 * HG):
-            at = (t // HG) * 16 + p * HG + t % HG
-            tail_rows[at : at + 1, :] = last[:, t * HD : (t + 1) * HD]
-    tail_out[...] = tail_rows[...].astype(BF16)
     pl.semaphore_wait(barrier, 8 + jnp.where(z > 0, 1, 0))
 
-    for d in (1, 3, 2):
-        send(
-            tail_out.at[pl.ds(pl.multiple_of(((x + d) % 4) * 16, 16), 16), :],
-            tail_in.at[pl.ds((4 - d) * 16, 16), :],
-            out_sem.at[8],
-            in_sem.at[1],
-            at_x(d),
-        )
-
-    for part, (lo, size) in enumerate(HALVES):
+    def send_heads(part):
+        lo, size = HALVES[part]
         for d in (2, 1, 3):
             send(
                 qkv_ref.at[:, pl.ds(0, ROWS), pl.ds(pl.multiple_of(((x + d) % 4) * GW + lo, 128), size)],
@@ -140,6 +124,8 @@
                 in_sem.at[8 + part],
                 at_x(d),
             )
+
+    send_heads(0)
     def own_piece(q, way, when):
         start = ((y + q) % 4) * QR
         send(
@@ -151,10 +137,28 @@
             when,
         )
 
-    for q in (0, 1):
-        own_piece(q, 0, None)
-        own_piece(q, 1, z > 0)
+    for r in (0, 1):
+        own_piece(r, 0, None)
+        own_piece(1 - r, 1, z > 0)
     send(w_ref, w_at(block_rows(zl, c), CW), out_sem.at[1], sib_sem.at[zl], sibling)
+
+    qkv_in.wait()
+    tail_rows[...] = jnp.zeros_like(tail_rows)
+    for p in range(3):
+        last = qkv_v[p, ROWS : ROWS + 1, :].astype(F32)
+        for t in range(4 * HG):
+            at = (t // HG) * 16 + p * HG + t % HG
+            tail_rows[at : at + 1, :] = last[:, t * HD : (t + 1) * HD]
+    tail_out[...] = tail_rows[...].astype(BF16)
+    for d in (2, 1, 3):
+        send(
+            tail_out.at[pl.ds(pl.multiple_of(((x + d) % 4) * 16, 16), 16), :],
+            tail_in.at[pl.ds((4 - d) * 16, 16), :],
+            out_sem.at[8],
+            in_sem.at[1],
+            at_x(d),
+        )
+    send_heads(1)
 
     def w_piece(k, q, way):
         b = (z + (8 - k if way == 0 else k)) % 8
@@ -164,27 +168,27 @@
         piece, _ = w_piece(k, q, way)
         send(piece, piece, out_sem.at[1], z_sem.at[way, 2 * k + 2 + q], at_z(1 if way == 0 else 15), when)
 
-    def w_step(k, q, late):
+    def w_step(k, r, late, only=None):
         todo = []
         for way in (0, 1):
-            if k == 4 and q != way:
-                continue
+            q = way if r == 0 else 1 - way
             crosses = (z if way == 0 else 15 - z) < k
             here = crosses if late else jnp.logical_not(crosses)
+            here = here if only is None else here & only
             piece, b = w_piece(k, q, way)
             pl.when(here)(lambda: arrived(piece, z_sem.at[way, 2 * k + q]))
-            if k < 3 or (k == 3 and q == way):
+            if k < 3 or (k == 3 and r == 0):
                 pass_on(k, q, way, here & (z > 0) if way == 1 and k < 3 and not late else here)
-            todo.append((piece, b, here))
-        for piece, b, here in todo:
+            todo.append((piece, b, q, here))
+        for piece, b, q, here in todo:
             send(piece, piece, out_sem.at[1], y_sem.at[q, b], at_y(1 if q == 0 else 3), here)
             send(piece, piece, out_sem.at[1], sib_sem.at[b], sibling, here)
 
     def w_back():
-        for q in (0, 1):
+        for q in (1, 0):
             own_piece(q, 1, z == 0)
         for k in (1, 2):
-            for q in (0, 1):
+            for q in (1, 0):
                 pass_on(k, q, 1, z == 0)
 
     def y_near(i):
@@ -224,9 +228,12 @@
     send(bsend, brecv, out_sem.at[2], in_sem.at[2], at_x(1))
 
     w_step(1, 0, False)
+    w_step(1, 1, False)
     gate_in.wait()
-    hot = lax.broadcasted_iota(jnp.int32, (16, 35), 1) == step_ref[0]
+    hot = lax.broadcasted_iota(jnp.int32, (16, 35), 1) == scalars[2]
     gate_row[...] = jnp.dot(hot.astype(F32).astype(BF16), gate_v[...], preferred_element_type=F32)
+
+    w_step(2, 0, False)
 
     own_heads.wait()
     arrived(tail_in.at[pl.ds(16, 48), :], in_sem.at[1])
@@ -266,7 +273,7 @@
         for j in range(4):
             for t in range(5):
                 tsend[j, i * 5 + t : i * 5 + t + 1, :] = value[MAIN + j : MAIN + j + 1, t * 128 : (t + 1) * 128]
-        if i >= CROSSING:
+        if i not in CROSSING:
             for d in (1, 3, 2):
                 send(terms.at[i, pl.ds(d * ROWS, ROWS), :], recv.at[4 - d, i], out_sem.at[3], term_sem.at[i], at_x(d))
             return
@@ -310,15 +317,13 @@
         arrived(packs.at[pl.ds(0, 3)], in_sem.at[6])
         chosen = jnp.zeros((32, 128), F32)
         for k in range(8):
-            chosen = jnp.where(source_ref[0] == k, packs[k % 4, k // 4].astype(F32), chosen)
+            chosen = jnp.where(scalars[1] == k, packs[k % 4, k // 4].astype(F32), chosen)
         patch[0:32, :] = chosen.astype(BF16)
         patch[32:64, :] = pltpu.roll(chosen, 64, 1).astype(BF16)
 
-    outs = []
-
     def finish(i):
         at = cols(i)
-        peers = (1, 3) if i < CROSSING else (1, 2, 3)
+        peers = (1, 3) if i in CROSSING else (1, 2, 3)
         arrived(recv.at[pl.ds(0, len(peers)), i], term_sem.at[i])
         projected = terms[i, 0:ROWS, :].astype(F32)
         for d in peers:
@@ -327,11 +332,10 @@
         projected = jnp.concatenate([projected, last], axis=0)
         condition = jnp.dot(patch[:, 0:64], embed_v[:, at], preferred_element_type=F32)[0 : ROWS + 1]
         out_v[i] = (
-            hidden_v[:, at].astype(F32) + reset_ref[0].astype(F32) * condition + gate_row[0:1, at] * projected
+            hidden_v[:, at].astype(F32) + scalars[0].astype(F32) * condition + gate_row[0:1, at] * projected
         ).astype(BF16)
-        copy = pltpu.make_async_copy(out_v.at[i], out_ref.at[:, at], loc_sem.at[len(locals_) + i])
+        copy = pltpu.make_async_copy(out_v.at[i], out_ref.at[:, at], loc_sem.at[len(locals_)])
         copy.start()
-        outs.append(copy)
 
     def send_tails(lo, size, k):
         tail_terms[:, lo : lo + size, :] = tsend[:, lo : lo + size, :].astype(BF16)
@@ -351,52 +355,50 @@
             value += trecv[d, lo : lo + size, :].astype(F32)
         tail_sum[lo : lo + size, :] = value
 
-    w_step(1, 1, False)
     attend(0)
-    w_step(2, 0, False)
     y_near(1)
     w_step(2, 1, False)
     w_step(1, 0, True)
     w_back()
     attend(1)
     own_w.wait()
+    edge = jnp.minimum(z, 15 - z)
     project(0)
     w_step(3, 0, False)
     pass_frame()
     w_step(1, 1, True)
     y_near(2)
+    w_step(2, 0, True, z != 0)
     project(1)
     w_step(3, 1, False)
-    w_step(2, 0, True)
+    w_step(2, 0, True, z == 0)
+    w_step(2, 1, True)
     y_near(3)
-    w_step(2, 1, True)
+    w_step(3, 0, True, edge >= 2)
     project(2)
-    add_on(0)
+    w_step(4, 0, False)
+    w_step(3, 0, True, edge < 2)
     y_near(4)
-    w_step(3, 0, True)
+    w_step(3, 1, True, edge >= 2)
     project(3)
-    add_on(1)
-    w_step(4, 0, False)
-    w_step(4, 1, False)
-    w_step(3, 1, True)
+    w_step(3, 1, True, edge < 2)
     y_near(5)
+    w_step(4, 0, True, edge >= 2)
     project(4)
-    add_on(2)
+    w_step(4, 0, True, edge < 2)
     pass_far()
-    w_step(4, 0, True)
-    w_step(4, 1, True)
+    add_on(3)
     y_near(6)
     project(5)
-    add_on(3)
+    add_on(4)
     y_near(7)
     project(6)
+    add_on(5)
     send_tails(0, 32, 7)
-    add_on(4)
-    pass_patches()
     project(7)
-    add_on(5)
     send_tails(32, 16, 10)
     add_on(6)
+    pass_patches()
     choose_patches()
     embed_in.wait()
     hidden_in.wait()
@@ -419,18 +421,16 @@
     left(packs.at[pl.ds(0, 3)], out_sem.at[6])
     left(trecv.at[pl.ds(1, 3)], out_sem.at[7])
     left(tail_in.at[pl.ds(16, 48), :], out_sem.at[8])
-    for copy in outs:
-        copy.wait()
+    pltpu.make_async_copy(out_v, out_v, loc_sem.at[len(locals_)]).wait()
 
 
 def per_device(qkv, hidden_in, clips, reset, source_group, step_index, conv_weight, embed_weight, out_weight, gate_table):
     anywhere = pl.BlockSpec(memory_space=pl.ANY)
-    scalar = pl.BlockSpec(memory_space=pltpu.SMEM)
     dma = pltpu.SemaphoreType.DMA
     result = pl.pallas_call(
         body,
         out_shape=jax.ShapeDtypeStruct((49, D), BF16),
-        in_specs=[scalar] * 3 + [anywhere] * 7,
+        in_specs=[pl.BlockSpec(memory_space=pltpu.SMEM)] + [anywhere] * 7,
         out_specs=anywhere,
         scratch_shapes=[
             pltpu.VMEM((3, 49, 4 * GW), BF16),
@@ -461,30 +461,33 @@
             pltpu.VMEM((2, 32, 128), BF16),
             pltpu.VMEM((16, D), F32),
             pltpu.VMEM((64, 128), BF16),
-            dma((16,)),
+            dma((9,)),
             dma((9,)),
             dma((2, 10)),
             dma((2, 8)),
             dma((8,)),
             dma((NB,)),
-            dma((CROSSING,)),
+            dma((NB,)),
             dma((11,)),
         ],
         compiler_params=pltpu.CompilerParams(
-            collective_id=0, has_side_effects=True, vmem_limit_bytes=63 * 1024 * 1024
+            collective_id=0, has_side_effects=True, vmem_limit_bytes=48 * 1024 * 1024
         ),
         cost_estimate=pl.CostEstimate(flops=2_000_000_000, bytes_accessed=8_000_000, transcendentals=400_000),
     )(
-        reset,
-        source_group,
-        step_index,
-        qkv[0].transpose(1, 0, 2),
-        hidden_in[0],
-        clips[0, 0],
-        conv_weight.transpose(0, 1, 2, 4, 3),
-        embed_weight,
-        out_weight.T,
-        gate_table,
+        jnp.concatenate([reset, source_group, step_index]),
+        *(
+            pltpu.with_memory_space_constraint(operand, pltpu.HBM)
+            for operand in (
+                qkv[0].transpose(1, 0, 2),
+                hidden_in[0],
+                clips[0, 0],
+                conv_weight.transpose(0, 1, 2, 4, 3),
+                embed_weight,
+                out_weight.T,
+                gate_table,
+            )
+        )
     )
     return result[None]
 

time: 53.6 us -> 50.4 us (0.940)
  the two profiles are of different devices: /device:TPU:32 before, /device:TPU:6 now
where the time goes in v4:
time: 50.4 us; the launch traced here: 50.3 us
  Pallas kernels  47.4 us (94%)
  between operations  1.95 us (4%)
  local copies, waits for them, and re-layouts  0.81 us (2%)
    pallas_call x1, Pallas kernels, per_device(): pl.pallas_call(body, out_shape=jax.ShapeDtypeStruct((49, D), BF16), in_sp...  47.4 us

profile of v4, /device:TPU:6, one launch (start us, length us, event | category | flops | bytes accessed | tf_op | source)
XLA Modules:
  0.0 50.3 jit_solution(17718193876558410040)
XLA Ops:
  1.9 0.1 pad_add_fusion.scalars
  2.0 47.4 %shard_map.100 = bf16[49,5120]{1,0:T(8,128)(2,1)S(1)} custom-call(s32[3]{0:T(128)S(1)} %pad_add_fusion.scalars, bf16[3,49,2560]{2,1,0:T(8,128)(2,1)} %bitcast.9, bf16[49,5120]{1,0:T(8,128)(2,1)} %bitcast.10, bf16[14,14,512]{2,1,0:T(8,128)(2,1)} %bitcast.13, bf16[2,3,3,16,512]{4,3,2,1,0:T(8,128)(2,1)} %bitcast.12, bf16[64,5120]{1,0:T(8,128)(2,1)} %embed_ref.1, ...), custom_call_target="tpu_custom_call" | custom-call | flops 2000000000 | bytes 8000000 | tf_op jit(solution)/shard_map/pallas_call | solution.py:430
  49.5 0.8 %copy.15 = bf16[1,49,5120]{2,1,0:T(8,128)(2,1)} copy(bf16[1,49,5120]{2,1,0:T(8,128)(2,1)S(1)} %bitcast.8) | data formatting | bytes 1003520

commit v5 on v4

--- a/solution.py
+++ b/solution.py
@@ -26,7 +26,7 @@
 
 
 def body(
-    scalars, qkv_ref, hidden_ref, clip_ref, conv_ref, embed_ref, w_ref, gate_ref,
+    reset_ref, source_ref, step_ref, qkv_ref, hidden_ref, clip_ref, conv_ref, embed_ref, w_ref, gate_ref,
     out_ref,
     qkv_v, hidden_v, clip_v, conv_v, embed_v, gate_v, out_v,
     wg, heads, tail_rows, tail_out, tail_in, att, terms, cross, recv, tsend, tail_terms, trecv, tail_sum, act, sh, bsend, brecv, packs, midway, gate_row, patch,
@@ -230,7 +230,7 @@
     w_step(1, 0, False)
     w_step(1, 1, False)
     gate_in.wait()
-    hot = lax.broadcasted_iota(jnp.int32, (16, 35), 1) == scalars[2]
+    hot = lax.broadcasted_iota(jnp.int32, (16, 35), 1) == step_ref[...]
     gate_row[...] = jnp.dot(hot.astype(F32).astype(BF16), gate_v[...], preferred_element_type=F32)
 
     w_step(2, 0, False)
@@ -317,7 +317,7 @@
         arrived(packs.at[pl.ds(0, 3)], in_sem.at[6])
         chosen = jnp.zeros((32, 128), F32)
         for k in range(8):
-            chosen = jnp.where(scalars[1] == k, packs[k % 4, k // 4].astype(F32), chosen)
+            chosen = jnp.where(source_ref[...] == k, packs[k % 4, k // 4].astype(F32), chosen)
         patch[0:32, :] = chosen.astype(BF16)
         patch[32:64, :] = pltpu.roll(chosen, 64, 1).astype(BF16)
 
@@ -332,7 +332,7 @@
         projected = jnp.concatenate([projected, last], axis=0)
         condition = jnp.dot(patch[:, 0:64], embed_v[:, at], preferred_element_type=F32)[0 : ROWS + 1]
         out_v[i] = (
-            hidden_v[:, at].astype(F32) + scalars[0].astype(F32) * condition + gate_row[0:1, at] * projected
+            hidden_v[:, at].astype(F32) + reset_ref[...].astype(F32) * condition + gate_row[0:1, at] * projected
         ).astype(BF16)
         copy = pltpu.make_async_copy(out_v.at[i], out_ref.at[:, at], loc_sem.at[len(locals_)])
         copy.start()
@@ -430,7 +430,7 @@
     result = pl.pallas_call(
         body,
         out_shape=jax.ShapeDtypeStruct((49, D), BF16),
-        in_specs=[pl.BlockSpec(memory_space=pltpu.SMEM)] + [anywhere] * 7,
+        in_specs=[pl.BlockSpec(memory_space=pltpu.VMEM)] * 3 + [anywhere] * 7,
         out_specs=anywhere,
         scratch_shapes=[
             pltpu.VMEM((3, 49, 4 * GW), BF16),
@@ -475,7 +475,9 @@
         ),
         cost_estimate=pl.CostEstimate(flops=2_000_000_000, bytes_accessed=8_000_000, transcendentals=400_000),
     )(
-        jnp.concatenate([reset, source_group, step_index]),
+        reset.reshape(1, 1),
+        source_group.reshape(1, 1),
+        step_index.reshape(1, 1),
         *(
             pltpu.with_memory_space_constraint(operand, pltpu.HBM)
             for operand in (

time: 50.4 us -> 49.8 us (0.988)
    pallas_call x1, Pallas kernels: 47.4 us -> 46.9 us  [per_device(): pl.pallas_call(body, out_shape=jax.ShapeDtypeStruct((49, D), BF16), in_sp...]
where the time goes in v5:
time: 49.8 us; the launch traced here: 49.7 us
  Pallas kernels  46.9 us (94%)
  between operations  1.95 us (4%)
  local copies, waits for them, and re-layouts  0.81 us (2%)
    pallas_call x1, Pallas kernels, per_device(): pl.pallas_call(body, out_shape=jax.ShapeDtypeStruct((49, D), BF16), in_sp...  46.9 us

profile of v5, /device:TPU:6, one launch (start us, length us, event | category | flops | bytes accessed | tf_op | source)
XLA Modules:
  0.0 49.7 jit_solution(4180973412681872586)
XLA Ops:
  1.9 46.9 %shard_map.100 = bf16[49,5120]{1,0:T(8,128)(2,1)S(1)} custom-call(s32[1,1]{1,0:T(1,128)} %bitcast.11.reset_ref, s32[1,1]{1,0:T(1,128)} %bitcast.12.source_ref, s32[1,1]{1,0:T(1,128)} %bitcast.13.step_ref, bf16[3,49,2560]{2,1,0:T(8,128)(2,1)} %bitcast.15, bf16[49,5120]{1,0:T(8,128)(2,1)} %bitcast.16, bf16[14,14,512]{2,1,0:T(8,128)(2,1)} %bitcast.19, ...), custom_call_target="tpu_custom_call" | custom-call | flops 2000000000 | bytes 8000000 | tf_op jit(solution)/shard_map/pallas_call | solution.py:430
  48.9 0.8 %copy.15 = bf16[1,49,5120]{2,1,0:T(8,128)(2,1)} copy(bf16[1,49,5120]{2,1,0:T(8,128)(2,1)S(1)} %bitcast.14) | data formatting | bytes 1003520

commit v6 on v5

--- a/solution.py
+++ b/solution.py
@@ -379,13 +379,11 @@
     w_step(4, 0, False)
     w_step(3, 0, True, edge < 2)
     y_near(4)
-    w_step(3, 1, True, edge >= 2)
+    w_step(3, 1, True)
     project(3)
-    w_step(3, 1, True, edge < 2)
     y_near(5)
-    w_step(4, 0, True, edge >= 2)
+    w_step(4, 0, True)
     project(4)
-    w_step(4, 0, True, edge < 2)
     pass_far()
     add_on(3)
     y_near(6)

time: 49.8 us -> 49.8 us (level)
  no operation moved by 1% of the time
where the time goes in v6:
time: 49.8 us; the launch traced here: 49.7 us
  Pallas kernels  46.9 us (94%)
  between operations  1.95 us (4%)
  local copies, waits for them, and re-layouts  0.81 us (2%)
    pallas_call x1, Pallas kernels, per_device(): pl.pallas_call(body, out_shape=jax.ShapeDtypeStruct((49, D), BF16), in_sp...  46.9 us

profile of v6, /device:TPU:6, one launch (start us, length us, event | category | flops | bytes accessed | tf_op | source)
XLA Modules:
  0.0 49.7 jit_solution(8856331390429194123)
XLA Ops:
  1.9 46.9 %shard_map.100 = bf16[49,5120]{1,0:T(8,128)(2,1)S(1)} custom-call(s32[1,1]{1,0:T(1,128)} %bitcast.11.reset_ref, s32[1,1]{1,0:T(1,128)} %bitcast.12.source_ref, s32[1,1]{1,0:T(1,128)} %bitcast.13.step_ref, bf16[3,49,2560]{2,1,0:T(8,128)(2,1)} %bitcast.15, bf16[49,5120]{1,0:T(8,128)(2,1)} %bitcast.16, bf16[14,14,512]{2,1,0:T(8,128)(2,1)} %bitcast.19, ...), custom_call_target="tpu_custom_call" | custom-call | flops 2000000000 | bytes 8000000 | tf_op jit(solution)/shard_map/pallas_call | solution.py:428
  48.9 0.8 %copy.15 = bf16[1,49,5120]{2,1,0:T(8,128)(2,1)} copy(bf16[1,49,5120]{2,1,0:T(8,128)(2,1)S(1)} %bitcast.14) | data formatting | bytes 1003520
